TPU v7x, 256 devices: a whole 4x4x8 slice. The times are simulated.
256 devices in a mesh: row: 32 (over y, z), col: 8 (over x, core).
Axes of the slice: x: 4, y: 4, z: 8, core: 2. Of those that a mesh axis runs over, the one named last changes fastest.
Arguments:
- panel: bfloat16 [131072, 2048], P('row'), as said below
- rhs: float32 [131072, 2048], P('row', 'col'), may hold values from -6 to 6
- block_slot: int32 [128], replicated, may hold values from 0 to 127, each once
- target: float32 [2, 1024], P(None, 'col'), may hold values from -0.125 to 0.125
Outputs:
- solved_rhs: float32 [131072, 2048], P('row', 'col')
- mean_part: float32 [2048], P('col')
Inputs may be any that keep to these rules, and one draw needn't show every extreme that they name: block_slot is a permutation of the storage slots. Within every tile of panel the diagonal entries lie between 1 and 3.
All inputs are finite; a program needn't handle non-finite values.
Results may differ from a plain program's by a relative error of at most 0.0034.
Values may be sent and summed in bfloat16 or wider, within the bound.
A program may use at most 128 MiB of HBM per device.

v0:
```python
import jax
import jax.numpy as jnp
from jax import lax
from jax.sharding import PartitionSpec as P

B = 1024


def from_root(shard, axis, root):
    mine = lax.axis_index(axis) == root
    return lax.psum(jnp.where(mine, shard, jnp.zeros_like(shard)), axis)


def send_solved(result, owner):
    return from_root(result, "row", owner)


def solve_pivot(panel, block_state, local, column):
    tile = lax.dynamic_slice_in_dim(panel, local * B, B, 0)[:, column * B : (column + 1) * B]
    result = lax.linalg.triangular_solve(
        jnp.tril(tile.astype(jnp.float32)), block_state, left_side=True, lower=True
    )
    return result.astype(jnp.bfloat16)


def apply_column(panel, state, order, column, solved):
    blocks_here = state.shape[0]
    term = jnp.dot(
        panel[:, column * B : (column + 1) * B], solved, preferred_element_type=jnp.float32
    )
    term = term.reshape(blocks_here, B, state.shape[2])
    return state - jnp.where((order > column)[:, None, None], term, 0.0)


def per_device(panel, rhs, block_slot, target):
    blocks_here = rhs.shape[0] // B
    width = rhs.shape[1]
    position = lax.axis_index("row")
    ramp = jnp.arange(block_slot.shape[0], dtype=jnp.int32)
    stored = position * blocks_here + jnp.arange(blocks_here, dtype=jnp.int32)
    order = jnp.sum(jnp.where(block_slot[None, :] == stored[:, None], ramp[None, :], 0), axis=1)
    state = rhs.reshape(blocks_here, B, width)
    owner_first = block_slot[0] // blocks_here
    local_first = block_slot[0] % blocks_here
    owner_second = block_slot[1] // blocks_here
    local_second = block_slot[1] % blocks_here
    first_state = lax.dynamic_index_in_dim(state, local_first, 0, keepdims=False)
    solved_first = send_solved(solve_pivot(panel, first_state, local_first, 0), owner_first)
    state = apply_column(panel, state, order, 0, solved_first)
    second_state = lax.dynamic_index_in_dim(state, local_second, 0, keepdims=False)
    solved_second = send_solved(solve_pivot(panel, second_state, local_second, 1), owner_second)
    state = apply_column(panel, state, order, 1, solved_second)
    first_wide = solved_first.astype(jnp.float32)
    second_wide = solved_second.astype(jnp.float32)
    final = jnp.where(
        (order == 0)[:, None, None],
        first_wide[None],
        jnp.where((order == 1)[:, None, None], second_wide[None], state),
    )
    gathered = lax.all_gather(target, "col", axis=1, tiled=True)
    mean_part = jnp.dot(gathered[0], first_wide, precision=lax.Precision.HIGHEST)
    mean_part = mean_part + jnp.dot(gathered[1], second_wide, precision=lax.Precision.HIGHEST)
    return (final.reshape(blocks_here * B, width), mean_part)


def solution(mesh):
    return jax.shard_map(
        per_device,
        mesh=mesh,
        in_specs=(P("row", None), P("row", "col"), P(), P(None, "col")),
        out_specs=(P("row", "col"), P("col")),
        check_vma=False,
    )
```

profile of v0, /device:TPU:6, one launch (start us, length us, event | category | flops | bytes accessed | tf_op | source)
XLA Modules:
  0.0 501.3 jit_solution(11214448440065231156)
XLA Ops:
  7.2 1.3 fusion.93
  13.1 6.7 %select_select_fusion = (f32[1024,1024]{1,0:T(8,128)}, f32[1024,1024]{1,0:T(8,128)}) fusion(bf16[4096,2048]{1,0:T(8,128)(2,1)} %param.6, s32[]{:T(128)S(6)} %select_n.90, s32[]{:T(128)S(6)} %add.51, s32[]{:T(128)S(6)} %select_n.83), kind=kLoop, calls=%fused_computation.14 | loop fusion | flops 7340032 | bytes 12582924 | tf_op jit(solution)/shard_map/triangular_solve/select.1 | solution.py:20
  19.8 22.5 %while.4 = (s32[]{:T(128)}, f32[1024,1024]{1,0:T(8,128)}, s32[8,2]{0,1:T(2,128)S(1)}, f32[8,128,128]{2,1,0:T(8,128)S(1)}, s32[]{:T(128)}) while((s32[]{:T(128)}, f32[1024,1024]{1,0:T(8,128)}, s32[8,2]{0,1:T(2,128)S(1)}, f32[8,128,128]{2,1,0:T(8,128)S(1)}, s32[]{:T(128)}) %tuple.93), condition=%wide.while_cond, body=%wide.while_body.sunk | while | flops 2 | bytes 131181 | solution.py:20
  20.5 2.2 bitcast_dynamic-update-slice_fusion.4
  23.3 2.2 bitcast_dynamic-update-slice_fusion.4
  26.1 2.2 bitcast_dynamic-update-slice_fusion.4
  28.9 2.2 bitcast_dynamic-update-slice_fusion.4
  31.8 2.2 bitcast_dynamic-update-slice_fusion.4
  34.6 2.2 bitcast_dynamic-update-slice_fusion.4
  37.4 2.2 bitcast_dynamic-update-slice_fusion.4
  40.2 2.1 bitcast_dynamic-update-slice_fusion.4
  42.4 78.6 %custom-call.4 = f32[8,128,128]{1,2,0:T(8,128)S(1)} custom-call(f32[8,128,128]{2,1,0:T(8,128)S(1)} %get-tuple-element.17), custom_call_target="InvertDiagBlocksLowerTriangular" | custom-call | tf_op jit(solution)/shard_map/triangular_solve/custom-call.1 | solution.py:20
  121.0 1.7 constant_dynamic-slice_fusion.2
  123.0 1.1 convolution_subtract_fusion.11
  124.4 1.2 convolution_subtract_fusion.7
  125.9 1.3 convolution_subtract_fusion.6
  127.6 1.4 convolution_subtract_fusion.5
  129.3 1.5 convolution_subtract_fusion.4
  131.1 1.5 convolution_subtract_fusion.10
  132.9 1.6 convolution_subtract_fusion.13
  134.9 0.9 convert_select_fusion.1
  136.3 23.1 %while.5 = (s32[]{:T(128)}, f32[1024,1024]{1,0:T(8,128)}, s32[8,2]{0,1:T(2,128)S(1)}, f32[8,128,128]{2,1,0:T(8,128)S(1)}, s32[]{:T(128)}) while((s32[]{:T(128)}, f32[1024,1024]{1,0:T(8,128)}, s32[8,2]{0,1:T(2,128)S(1)}, f32[8,128,128]{2,1,0:T(8,128)S(1)}, s32[]{:T(128)}) %tuple.103), condition=%wide.while_cond.clone, body=%wide.while_body.clone.sunk | while | flops 2 | bytes 131181 | solution.py:20
  136.4 0.6 fusion.123
  137.0 2.2 bitcast_dynamic-update-slice_fusion.5
  139.3 0.6 fusion.123
  139.9 2.2 bitcast_dynamic-update-slice_fusion.5
  142.2 0.6 fusion.123
  142.8 2.2 bitcast_dynamic-update-slice_fusion.5
  145.1 0.6 fusion.123
  145.7 2.2 bitcast_dynamic-update-slice_fusion.5
  148.0 0.6 fusion.123
  148.6 2.2 bitcast_dynamic-update-slice_fusion.5
  150.9 0.6 fusion.123
  151.5 2.2 bitcast_dynamic-update-slice_fusion.5
  153.8 0.6 fusion.123
  154.4 2.2 bitcast_dynamic-update-slice_fusion.5
  156.7 0.6 fusion.123
  157.3 2.2 bitcast_dynamic-update-slice_fusion.5
  160.1 0.8 copy.17
  161.2 0.6 dynamic-slice.7
  161.8 78.6 %custom-call.5 = f32[8,128,128]{1,2,0:T(8,128)S(1)} custom-call(f32[8,128,128]{2,1,0:T(8,128)S(1)} %get-tuple-element.18), custom_call_target="InvertDiagBlocksLowerTriangular" | custom-call | tf_op jit(solution)/shard_map/triangular_solve/custom-call.1 | solution.py:20
  240.4 46.9 %all-reduce.3.cloned.1.call-done = bf16[1024,256]{1,0:T(8,128)(2,1)} async-done(((bf16[1024,256]{1,0:T(8,128)(2,1)}), bf16[1024,256]{1,0:T(8,128)(2,1)}) %all-reduce.3.cloned.1.call-update) | async-done | bytes 524304 | tf_op jit(solution)/shard_map/psum | solution.py:11
  287.3 7.9 %fusion.4 = f32[4096,256]{0,1:T(8,128)} fusion(bf16[1024,256]{1,0:T(8,128)(2,1)} %all-reduce.3.cloned.1.call-done, bf16[4096,2048]{1,0:T(8,128)(2,1)} %param.6), kind=kOutput, calls=%fused_computation.8 | convolution fusion | flops 2147483648 | bytes 13107200 | tf_op jit(solution)/shard_map/dot_general | solution.py:28
  295.2 6.3 %reshape.62 = f32[4,1024,256]{1,0,2:T(4,128)} reshape(f32[4096,256]{0,1:T(8,128)} %fusion.4) | data formatting | bytes 8388608 | tf_op jit(solution)/shard_map/reshape | solution.py:31
  301.5 4.3 fusion.22
  306.3 1.2 convolution_subtract_fusion.9
  307.9 1.5 convolution_subtract_fusion.3
  309.7 1.8 convolution_subtract_fusion.2
  311.8 2.0 convolution_subtract_fusion.1
  314.1 2.2 convolution_subtract_fusion
  316.6 2.4 convolution_subtract_fusion.8
  319.4 2.7 convolution_subtract_fusion.12
  322.4 0.8 convert_select_fusion
  323.3 5.7 %copy.14 = f32[4096,256]{0,1:T(8,128)} copy(f32[4096,256]{1,0:T(8,128)} %param.7) | data formatting | bytes 8388608 | tf_op args[1]
  329.1 7.7 %all_gather.3 = f32[2,1024]{1,0:T(2,128)S(1)} all-gather(f32[2,128]{1,0:T(2,128)S(1)} %copy-done.5), channel_id=1, replica_groups=mesh['row'=32,'col'=8] {'col'}, dimensions={1}, use_global_device_ids=true | all-gather | bytes 9216 | tf_op jit(solution)/shard_map/all_gather | solution.py:60
  337.0 1.2 broadcast_in_dim.102
  338.2 5.8 %copy.19 = f32[32,8,4,1024]{3,1,2,0:T(8,128)} copy(f32[32,8,4,1024]{3,2,1,0:T(4,128)S(1)} %bitcast.180) | data formatting | bytes 8388608
  344.3 123.5 %all-reduce.5.cloned.1.call-done = bf16[1024,256]{1,0:T(8,128)(2,1)} async-done(((bf16[1024,256]{1,0:T(8,128)(2,1)}), bf16[1024,256]{1,0:T(8,128)(2,1)}) %all-reduce.5.cloned.1.call-update) | async-done | bytes 524304 | tf_op jit(solution)/shard_map/psum | solution.py:11
  467.9 1.2 copy.13
  469.1 1.2 broadcast_in_dim.109
  470.3 5.9 %copy.21 = f32[32,8,4,1024]{3,1,2,0:T(8,128)} copy(f32[32,8,4,1024]{3,2,1,0:T(4,128)S(1)} %bitcast.181) | data formatting | bytes 8388608
  476.2 11.5 %fusion.19 = f32[4096,256]{0,1:T(8,128)} fusion(f32[4096,256]{0,1:T(8,128)} %bitcast.182, f32[4096,256]{0,1:T(8,128)} %bitcast.183, bf16[1024,256]{1,0:T(8,128)(2,1)S(1)} %copy-done.2, bf16[4096,2048]{1,0:T(8,128)(2,1)} %param.6, f32[4096,256]{0,1:T(8,128)S(1)} %copy-done.1, f32[4096,256]{0,1:T(8,128)S(1)} %copy-done, pred[4096]{0:T(1024)(128)(4,1)S(1)} %bitcast.193, ...), kind=kOutput, calls=%fused_computation.13 | convolution fusion | flops 2153775104 | bytes 29900800 | tf_op jit(solution)/shard_map/dot_general | solution.py:28
  487.8 5.6 %copy.15 = f32[4096,256]{1,0:T(8,128)} copy(f32[4096,256]{0,1:T(8,128)} %fusion.19) | data formatting | bytes 8388608
  493.7 0.6 add.48
  (73 shorter events, 12.6 us)
Async XLA Ops:
  7.2 280.1 %all-reduce.3.cloned.1.call-start = ((), (), s32[]{:S(2)}) async-start(), calls=%async_computation | async-start | bytes 1048576 | tf_op jit(solution)/shard_map/psum | solution.py:11
  131.1 29.9 %copy-start.4 = (s32[128]{0:T(128)S(1)}, s32[128]{0:T(128)}, u32[]{:S(2)}) copy-start(s32[128]{0:T(128)} %param.8) | copy-start | bytes 1540
  135.8 332.1 %all-reduce.5.cloned.1.call-start = ((), (), s32[]{:S(2)}) async-start(), calls=%async_computation.1 | async-start | bytes 1048576 | tf_op jit(solution)/shard_map/psum | solution.py:11
  323.3 5.8 %copy-start.5 = (f32[2,128]{1,0:T(2,128)S(1)}, f32[2,128]{1,0:T(2,128)}, u32[]{:S(2)}) copy-start(f32[2,128]{1,0:T(2,128)} %param.9) | copy-start | bytes 3076
  323.3 13.5 %copy-start.3 = (bf16[1024,256]{1,0:T(8,128)(2,1)S(1)}, bf16[1024,256]{1,0:T(8,128)(2,1)}, u32[]{:S(2)}) copy-start(bf16[1024,256]{1,0:T(8,128)(2,1)} %all-reduce.3.cloned.1.call-done) | copy-start | bytes 1572868
  469.1 7.1 %copy-start.2 = (bf16[1024,256]{1,0:T(8,128)(2,1)S(1)}, bf16[1024,256]{1,0:T(8,128)(2,1)}, u32[]{:S(2)}) copy-start(bf16[1024,256]{1,0:T(8,128)(2,1)} %all-reduce.5.cloned.1.call-done) | copy-start | bytes 1572868
  470.3 5.9 %copy-start = (f32[4096,256]{0,1:T(8,128)S(1)}, f32[4096,256]{0,1:T(8,128)}, u32[]{:S(2)}) copy-start(f32[4096,256]{0,1:T(8,128)} %fusion.4) | copy-start | bytes 12582916
  470.3 5.9 %copy-start.1 = (f32[4096,256]{0,1:T(8,128)S(1)}, f32[4096,256]{0,1:T(8,128)}, u32[]{:S(2)}) copy-start(f32[4096,256]{0,1:T(8,128)} %copy.14) | copy-start | bytes 12582916
Sparse Core Ops, SparseCore 0:
  135.9 151.3 all-reduce.2
  323.3 144.4 all-reduce.4
where the time goes:
time: 509 us; the launch traced here: 501 us
  other arithmetic  171 us (34%)
  waiting for transfers between devices  170 us (33%)
  local copies, waits for them, and re-layouts  83.3 us (16%)
  matrix products  48.4 us (10%)
  between operations  20 us (4%)
  blocking collectives  7.66 us (2%)
    psum x2, waiting for transfers between devices, from_root(): return lax.psum(jnp.where(mine, shard, jnp.zeros_like(shard)), axis)  170 us
    another operation x4, other arithmetic, solve_pivot(): lax.linalg.triangular_solve(jnp.tril(tile.astype(jnp.float32)), block_sta...  164 us
    another operation x51, local copies, waits for them, and re-layouts, solve_pivot(): lax.linalg.triangular_solve(jnp.tril(tile.astype(jnp.float32)), block_sta...  45.4 us
    another operation x30, matrix products, solve_pivot(): lax.linalg.triangular_solve(jnp.tril(tile.astype(jnp.float32)), block_sta...  28.3 us
    unnamed x24, local copies, waits for them, and re-layouts  24.2 us
    dot_general x2, matrix products, apply_column(): jnp.dot(panel[:, column * B:(column + 1) * B], solved, preferred_element_...  19.4 us
  transfers between devices with their start and end apart: 2, of which 2 were waited for; matrix products, arithmetic and copies ran while one was open for 23% of the time, Pallas kernels for 0%

commit v1 on v0

v1 whole, which is shorter than its diff:
```python
import functools

import jax
import jax.numpy as jnp
from jax import lax
from jax.experimental import pallas as pl
from jax.experimental.pallas import tpu as pltpu
from jax.sharding import PartitionSpec as P

B = 1024
W = 256
NY, NZ, NC = 4, 8, 8
CH = 256
NCH = B // CH
BASE = 16
F32, BF16 = jnp.float32, jnp.bfloat16
MESH = pl.DeviceIdType.MESH


def dot(a, b):
    return jnp.dot(a, b, preferred_element_type=F32)


def split(x):
    hi = x.astype(BF16)
    return hi, (x - hi.astype(F32)).astype(BF16)


def iota(shape, dim):
    return lax.broadcasted_iota(jnp.int32, shape, dim)


def spread_matrix():
    shape = (128, BASE * 128)
    lane = iota(shape, 1)
    return jnp.where(iota(shape, 0) == (lane % 128) // BASE * BASE + lane // 128, 1.0, 0.0).astype(BF16)


def invert_small(blocks, spread):
    groups = len(blocks)
    lane = iota((BASE, 128), 1)
    packed = []
    for block in blocks:
        wide = block.astype(F32)
        acc = jnp.zeros((BASE, 128), F32)
        for b in range(128 // BASE):
            acc = jnp.where(lane // BASE == b, wide[BASE * b : BASE * (b + 1)], acc)
        packed.append(acc)
    packed = jnp.concatenate(packed, axis=0).astype(BF16)
    factors = dot(packed, spread)
    part = [factors[:, 128 * j : 128 * (j + 1)].reshape(groups, BASE, 128) for j in range(BASE)]
    row = iota((groups, BASE, 128), 1)
    diag = part[0]
    for j in range(1, BASE):
        diag = jnp.where(row == j, part[j], diag)
    scale = 1.0 / diag
    x = jnp.where(iota((groups, BASE, 128), 2) % BASE == row, scale, 0.0)
    for j in range(BASE - 1):
        factor = jnp.where(row > j, part[j] * scale, 0.0)
        x = x - factor * x[:, j : j + 1, :]
    return [x[g] for g in range(groups)]


def join_inverses(diag_block):
    groups = B // 128
    spread = spread_matrix()
    blocks = [diag_block(g) for g in range(groups)]
    small = invert_small(blocks, spread)
    r, c = iota((128, 128), 0), iota((128, 128), 1)
    inverses = []
    for g in range(groups):
        tiled = jnp.concatenate([small[g]] * (128 // BASE), axis=0)
        inverses.append(jnp.where(r // BASE == c // BASE, tiled, 0.0))
    size = BASE
    while size < 128:
        mask = ((r // size) % 2 == 1) & (c // size == r // size - 1)
        for g in range(groups):
            off = jnp.where(mask, blocks[g], jnp.zeros_like(blocks[g]))
            hi, lo = split(inverses[g])
            t = dot(jnp.concatenate([off, off], axis=1), jnp.concatenate([hi, lo], axis=0))
            thi, tlo = split(t)
            u = dot(jnp.concatenate([hi, lo], axis=1), jnp.concatenate([thi, thi], axis=0)) + dot(hi, tlo)
            inverses[g] = inverses[g] - u
        size *= 2
    return inverses


def whole_inverse(inverses, corner, b):
    first, second = inverses[2 * b], inverses[2 * b + 1]
    hi, lo = split(first)
    t = dot(jnp.concatenate([corner, corner], axis=1), jnp.concatenate([hi, lo], axis=0))
    thi, tlo = split(t)
    hi2, lo2 = split(second)
    u = dot(jnp.concatenate([hi2, lo2], axis=1), jnp.concatenate([thi, thi], axis=0)) + dot(hi2, tlo)
    full = jnp.concatenate(
        [
            jnp.concatenate([first, jnp.zeros((128, 128), F32)], axis=1),
            jnp.concatenate([-u, second], axis=1),
        ],
        axis=0,
    )
    return split(full)


def kernel(
    slot_ref, target_ref, panel_hbm, rhs_hbm,
    out_hbm, mean_ref,
    panel_0, panel_1, state, diag_0, diag_1, work, inv_hi, inv_lo, solved, x_send, y_recv, z_send, z_recv, gathered, tgt,
    load_sem, store_sem, send_sem, recv_sem, tgt_send, tgt_recv,
):
    row, col = lax.axis_index("row"), lax.axis_index("col")
    y, z = row // NZ, row % NZ
    y_peers = [(lax.rem(y + d, NY) * NZ + z, col) for d in range(1, NY)]
    z_peers = [(y * NZ + lax.rem(z + d, NZ), col) for d in range(1, NZ)]
    c_peers = [(row, lax.rem(col + d, NC)) for d in range(1, NC)]
    tgt[...] = jnp.zeros_like(tgt)
    tgt[col, 0:2, :] = target_ref[...]
    barrier = pltpu.get_barrier_semaphore()
    for peer in y_peers + z_peers + c_peers:
        pl.semaphore_signal(barrier, inc=1, device_id=peer, device_id_type=MESH)

    def load(src, dst, k):
        copy = pltpu.make_async_copy(src, dst, load_sem.at[k])
        copy.start()
        return copy

    blocks = 4
    panel, diag = [panel_0, panel_1], [diag_0, diag_1]

    def load_diag(k, sem):
        for t in range(blocks):
            for b in range(NCH):
                load(
                    panel_hbm.at[pl.ds(t * B + b * CH, CH), pl.ds(k * B + b * CH, CH)],
                    diag[k].at[t, pl.ds(b * CH, CH)],
                    sem,
                )

    def load_column(k, sem):
        for t in range(blocks):
            load(panel_hbm.at[pl.ds(t * B, B), pl.ds(k * B, B)], panel[k].at[t], sem)

    load_diag(0, 0)
    for t in range(blocks):
        load(rhs_hbm.at[pl.ds(t * B, B)], state.at[t], 1)
    load_column(0, 2)
    load_diag(1, 3)
    load_column(1, 4)

    mine = [slot_ref[0] // blocks == row, slot_ref[1] // blocks == row]
    local = [slot_ref[0] % blocks, slot_ref[1] % blocks]

    def wait_load(ref, k):
        pltpu.make_async_copy(ref, ref, load_sem.at[k]).wait()

    def invert(k):
        found = join_inverses(
            lambda g: diag[k][local[k], pl.ds(128 * g, 128), pl.ds(128 * (g % 2), 128)]
        )
        for b in range(NCH):
            corner = diag[k][local[k], pl.ds(256 * b + 128, 128), pl.ds(0, 128)]
            inv_hi[b], inv_lo[b] = whole_inverse(found, corner, b)

    def send(src, dst, k, c, stage, peer):
        pltpu.make_async_remote_copy(
            src_ref=src, dst_ref=dst, send_sem=send_sem.at[k, c, stage], recv_sem=recv_sem.at[k, c, stage],
            device_id=peer, device_id_type=MESH,
        ).start()

    def solve(k):
        his, los = [], []
        for b in range(NCH):
            part = work[pl.ds(b * CH, CH), :]
            for a in range(b):
                tile = panel[k][local[k], pl.ds(b * CH, CH), pl.ds(a * CH, CH)]
                part = part - (dot(tile, his[a]) + dot(tile, los[a]))
            hi, lo = split(part)
            ihi, ilo = inv_hi[b], inv_lo[b]
            x = dot(ihi, hi) + (dot(ihi, lo) + dot(ilo, hi))
            hi, lo = split(x)
            his.append(hi)
            los.append(lo)
            masked = jnp.where(mine[k], x, 0.0).astype(BF16)
            for j in range(NY):
                for i in range(NZ):
                    r = 64 * j + 16 * (i // 2)
                    x_send[k, b, j, i] = masked[r : r + 16, 128 * (i % 2) : 128 * (i % 2 + 1)]
            if k == 0 and b == 0:
                pl.semaphore_wait(barrier, NY + NZ + NC - 3)
                for peer in c_peers:
                    pltpu.make_async_remote_copy(
                        src_ref=tgt.at[col], dst_ref=tgt.at[col], send_sem=tgt_send, recv_sem=tgt_recv,
                        device_id=peer, device_id_type=MESH,
                    ).start()
            for d in range(1, NY):
                send(x_send.at[k, b, lax.rem(y + d, NY)], y_recv.at[k, b, d], k, b, 0, y_peers[d - 1])

    def arrived(ref, k, c, stage):
        pltpu.make_async_copy(ref, ref, recv_sem.at[k, c, stage]).wait()

    def reduce_y(k, c):
        arrived(y_recv.at[k, c, pl.ds(1, NY - 1)], k, c, 0)
        z_send[k, c] = (x_send[k, c, y] + y_recv[k, c, 1]) + (y_recv[k, c, 2] + y_recv[k, c, 3])
        for d in range(1, NZ):
            send(z_send.at[k, c, lax.rem(z + d, NZ)], z_recv.at[k, c, d], k, c, 1, z_peers[d - 1])

    def reduce_z(k, c):
        arrived(z_recv.at[k, c, pl.ds(1, NZ - 1)], k, c, 1)
        total = z_send[k, c, z]
        for d in range(1, NZ):
            total = total + z_recv[k, c, d]
        gathered[k, c, y, z] = total
        piece = gathered.at[k, c, y, z]
        for d in range(1, NZ):
            send(piece, piece, k, c, 2, z_peers[d - 1])

    def gather_z(k, c):
        arrived(z_recv.at[k, c, pl.ds(1, NZ - 1)], k, c, 2)
        piece = gathered.at[k, c, y]
        for d in range(1, NY):
            send(piece, piece, k, c, 3, y_peers[d - 1])

    def gather_y(k, c):
        arrived(y_recv.at[k, c, pl.ds(1, NY - 1)], k, c, 3)
        for j in range(NY):
            for i in range(NZ):
                r = 64 * j + 16 * (i // 2)
                solved[k, pl.ds(c * CH + r, 16), pl.ds(128 * (i % 2), 128)] = gathered[k, c, j, i]

    wait_load(diag_0, 0)
    invert(0)
    wait_load(state, 1)
    work[...] = state[local[0]]
    wait_load(panel_0, 2)
    solve(0)
    for c in range(NCH):
        reduce_y(0, c)
    wait_load(diag_1, 3)
    invert(1)
    for c in range(NCH):
        reduce_z(0, c)
    for c in range(NCH):
        gather_z(0, c)
    wait_load(panel_1, 4)
    work[...] = state[local[1]]
    for c in range(NCH):
        gather_y(0, c)
        work[...] = work[...] - dot(panel_0[local[1], :, pl.ds(c * CH, CH)], solved[0, pl.ds(c * CH, CH), :])
    solve(1)

    first_here = [slot_ref[0] == row * blocks + t for t in range(blocks)]
    second_here = [slot_ref[1] == row * blocks + t for t in range(blocks)]

    tile_rows = 256

    def apply_first(t, i):
        rows = pl.ds(pl.multiple_of(i * tile_rows, tile_rows), tile_rows)
        term = dot(panel_0[t, rows, :], solved[0])
        state[t, rows, :] = state[t, rows, :] - term

    def apply_second(t, i):
        rows = pl.ds(pl.multiple_of(i * tile_rows, tile_rows), tile_rows)
        term = dot(panel_1[t, rows, :], solved[1])
        value = state[t, rows, :] - term
        value = jnp.where(second_here[t], solved[1, rows, :].astype(F32), value)
        state[t, rows, :] = jnp.where(first_here[t], solved[0, rows, :].astype(F32), value)
        pltpu.make_async_copy(
            state.at[t, rows], out_hbm.at[pl.ds(t * B + pl.multiple_of(i * tile_rows, tile_rows), tile_rows)], store_sem
        ).start()

    for c in range(NCH):
        reduce_y(1, c)
    for t in range(2):
        lax.fori_loop(0, B // tile_rows, lambda i, _: apply_first(t, i), None)
    for c in range(NCH):
        reduce_z(1, c)
    for t in range(2, 4):
        lax.fori_loop(0, B // tile_rows, lambda i, _: apply_first(t, i), None)
    for c in range(NCH):
        gather_z(1, c)
    pltpu.make_async_copy(tgt.at[pl.ds(0, NC - 1)], tgt.at[pl.ds(0, NC - 1)], tgt_recv).wait()
    for c in range(NCH):
        gather_y(1, c)
    for t in range(blocks):
        lax.fori_loop(0, B // tile_rows, lambda i, _: apply_second(t, i), None)

    mean = jnp.zeros((8, W), F32)
    for d in range(NC):
        rest = tgt[d]
        for _ in range(3):
            piece = rest.astype(BF16)
            rest = rest - piece.astype(F32)
            wide = jnp.concatenate([piece, jnp.zeros_like(piece)], axis=0)
            for k in range(2):
                found = dot(wide, solved[k, pl.ds(128 * d, 128), :])
                mean = mean + jnp.where(iota((8, W), 0) == k, found[0:8], 0.0)
    mean_ref[...] = mean[0:1] + mean[1:2]

    for k in range(2):
        for c in range(NCH):
            for stage, ref in enumerate((y_recv, z_recv, z_recv, y_recv)):
                count = (NY if stage in (0, 3) else NZ) - 1
                sent = ref.at[k, c, pl.ds(1, count)]
                pltpu.make_async_copy(sent, sent, send_sem.at[k, c, stage]).wait()
    pltpu.make_async_copy(tgt.at[pl.ds(0, NC - 1)], tgt.at[pl.ds(0, NC - 1)], tgt_send).wait()
    pltpu.make_async_copy(state, state, store_sem).wait()


def per_device(panel, rhs, block_slot, target):
    rows, width = rhs.shape
    piece = (NY, NZ, 16, 128)
    out, mean = pl.pallas_call(
        kernel,
        out_shape=(jax.ShapeDtypeStruct((rows, width), F32), jax.ShapeDtypeStruct((1, width), F32)),
        in_specs=[
            pl.BlockSpec(memory_space=pltpu.SMEM),
            pl.BlockSpec(memory_space=pltpu.VMEM),
            pl.BlockSpec(memory_space=pl.ANY),
            pl.BlockSpec(memory_space=pl.ANY),
        ],
        out_specs=(pl.BlockSpec(memory_space=pl.ANY), pl.BlockSpec(memory_space=pltpu.VMEM)),
        scratch_shapes=[
            pltpu.VMEM((4, B, B), BF16),
            pltpu.VMEM((4, B, B), BF16),
            pltpu.VMEM((4, B, W), F32),
            pltpu.VMEM((4, B, CH), BF16),
            pltpu.VMEM((4, B, CH), BF16),
            pltpu.VMEM((B, W), F32),
            pltpu.VMEM((NCH, CH, CH), BF16),
            pltpu.VMEM((NCH, CH, CH), BF16),
            pltpu.VMEM((2, B, W), BF16),
            pltpu.VMEM((2, NCH) + piece, BF16),
            pltpu.VMEM((2, NCH) + piece, BF16),
            pltpu.VMEM((2, NCH) + piece[1:], BF16),
            pltpu.VMEM((2, NCH) + piece[1:], BF16),
            pltpu.VMEM((2, NCH) + piece, BF16),
            pltpu.VMEM((NC, 8, 128), F32),
            pltpu.SemaphoreType.DMA((5,)),
            pltpu.SemaphoreType.DMA,
            pltpu.SemaphoreType.DMA((2, NCH, 4)),
            pltpu.SemaphoreType.DMA((2, NCH, 4)),
            pltpu.SemaphoreType.DMA,
            pltpu.SemaphoreType.DMA,
        ],
        compiler_params=pltpu.CompilerParams(
            collective_id=0, has_side_effects=True, vmem_limit_bytes=56 * 2**20
        ),
        name="substitute",
    )(block_slot, target, panel, rhs)
    return out, mean.reshape(width)


def solution(mesh):
    return jax.shard_map(
        per_device,
        mesh=mesh,
        in_specs=(P("row", None), P("row", "col"), P(), P(None, "col")),
        out_specs=(P("row", "col"), P("col")),
        check_vma=False,
    )
```

time: 509 us -> 72.3 us (0.14); the launches traced: 501 us -> 72.2 us
  other arithmetic: 171 us -> 0 us
  waiting for transfers between devices: 170 us -> 0 us
  local copies, waits for them, and re-layouts: 83.3 us -> 5.04 us
  Pallas kernels: 0 us -> 66.5 us
  matrix products: 48.4 us -> 0 us
  between operations: 20 us -> 0.65 us
  blocking collectives: 7.66 us -> 0 us
    psum x2 -> x0, waiting for transfers between devices: 170 us -> none  [from_root(): return lax.psum(jnp.where(mine, shard, jnp.zeros_like(shard)), axis)]
    another operation x4 -> x0, other arithmetic: 164 us -> none  [solve_pivot(): lax.linalg.triangular_solve(jnp.tril(tile.astype(jnp.float32)), block_sta...]
    pallas_call x0 -> x1, Pallas kernels: none -> 66.5 us  [per_device(): pl.pallas_call(kernel, out_shape=(jax.ShapeDtypeStruct((rows, width), F32...]
    another operation x51 -> x0, local copies, waits for them, and re-layouts: 45.4 us -> none  [solve_pivot(): lax.linalg.triangular_solve(jnp.tril(tile.astype(jnp.float32)), block_sta...]
    another operation x30 -> x0, matrix products: 28.3 us -> none  [solve_pivot(): lax.linalg.triangular_solve(jnp.tril(tile.astype(jnp.float32)), block_sta...]
    dot_general x4 -> x0, matrix products: 20.1 us -> none  [the longest x2 19.4 us: apply_column(): jnp.dot(panel[:, column * B:(column + 1) * B], solved, preferred_element_...]
    unnamed x24 -> x4, local copies, waits for them, and re-layouts: 24.2 us -> 5.04 us
    all_gather x1 -> x0, blocking collectives: 7.66 us -> none  [per_device(): gathered = lax.all_gather(target, 'col', axis=1, tiled=True)]
  transfers between devices with their start and end apart: 2 -> 0, of which waited for: 2 -> 0; matrix products, arithmetic and copies ran while one was open for 23% -> 0% of each run, Pallas kernels for 0% -> 0%
where the time goes in v1:
time: 72.3 us; the launch traced here: 72.2 us
  Pallas kernels  66.5 us (92%)
  local copies, waits for them, and re-layouts  5.04 us (7%)
    pallas_call x1, Pallas kernels, per_device(): pl.pallas_call(kernel, out_shape=(jax.ShapeDtypeStruct((rows, width), F32...  66.5 us
    unnamed x4, local copies, waits for them, and re-layouts  5.04 us

profile of v1, /device:TPU:6, one launch (start us, length us, event | category | flops | bytes accessed | tf_op | source)
XLA Modules:
  0.0 72.2 jit_solution(5939200052302233455)
XLA Ops:
  0.6 66.5 %substitute.1 = (f32[4096,256]{1,0:T(8,128)}, f32[1,256]{1,0:T(1,128)}) custom-call(s32[128]{0:T(128)} %slot_ref.1, f32[2,128]{1,0:T(2,128)} %target_ref.1, bf16[4096,2048]{1,0:T(8,128)(2,1)} %panel_hbm.1, f32[4096,256]{1,0:T(8,128)} %rhs_hbm.1), custom_call_target="tpu_custom_call" | custom-call | tf_op jit(solution)/shard_map/substitute/pallas_call | solution.py:312
  67.1 0.0 copy-start
  67.1 4.5 %copy.8 = f32[4096,256]{1,0:T(8,128)} copy(f32[4096,256]{1,0:T(8,128)} %get-tuple-element.8) | data formatting | bytes 8388608
  71.6 0.0 copy-done
  71.6 0.6 copy.9
Async XLA Ops:
  67.1 4.5 %copy-start = (f32[1,256]{1,0:T(1,128)S(1)}, f32[1,256]{1,0:T(1,128)}, u32[]{:S(2)}) copy-start(f32[1,256]{1,0:T(1,128)} %get-tuple-element.5) | copy-start | bytes 3076

commit v2 on v1

--- a/solution.py
+++ b/solution.py
@@ -73,40 +73,77 @@
         inverses.append(jnp.where(r // BASE == c // BASE, tiled, 0.0))
     size = BASE
     while size < 128:
-        mask = ((r // size) % 2 == 1) & (c // size == r // size - 1)
-        for g in range(groups):
-            off = jnp.where(mask, blocks[g], jnp.zeros_like(blocks[g]))
-            hi, lo = split(inverses[g])
-            t = dot(jnp.concatenate([off, off], axis=1), jnp.concatenate([hi, lo], axis=0))
-            thi, tlo = split(t)
-            u = dot(jnp.concatenate([hi, lo], axis=1), jnp.concatenate([thi, thi], axis=0)) + dot(hi, tlo)
-            inverses[g] = inverses[g] - u
+        odd = [slice(i, i + size) for i in range(size, 128, 2 * size)]
+        mask = (c // size == r // size - 1) & ((r // size) % 2 == 1)
+        off = [rows_of(jnp.where(mask, block, jnp.zeros_like(block)), odd) for block in blocks]
+        inverses = joined(inverses, off, odd)
         size *= 2
     return inverses
 
 
-def whole_inverse(inverses, corner, b):
-    first, second = inverses[2 * b], inverses[2 * b + 1]
-    hi, lo = split(first)
-    t = dot(jnp.concatenate([corner, corner], axis=1), jnp.concatenate([hi, lo], axis=0))
-    thi, tlo = split(t)
-    hi2, lo2 = split(second)
-    u = dot(jnp.concatenate([hi2, lo2], axis=1), jnp.concatenate([thi, thi], axis=0)) + dot(hi2, tlo)
-    full = jnp.concatenate(
-        [
-            jnp.concatenate([first, jnp.zeros((128, 128), F32)], axis=1),
-            jnp.concatenate([-u, second], axis=1),
-        ],
-        axis=0,
-    )
-    return split(full)
+def rows_of(x, parts):
+    return jnp.concatenate([x[p] for p in parts], axis=0)
+
+
+def joined(inverses, off, odd):
+    size = odd[0].stop - odd[0].start
+    parts = [split(x) for x in inverses]
+    low = [(rows_of(hi, odd), rows_of(lo, odd)) for hi, lo in parts]
+    t = [split(dot(jnp.concatenate([e, e], axis=1), jnp.concatenate(p, axis=0))) for e, p in zip(off, parts)]
+
+    def spread_rows(x):
+        gap = jnp.zeros((size, x.shape[1]), x.dtype)
+        return jnp.concatenate([v for i in range(len(odd)) for v in (gap, x[size * i : size * (i + 1)])], axis=0)
+
+    t = [(spread_rows(hi), spread_rows(lo)) for hi, lo in t]
+    u = [
+        dot(jnp.concatenate([p[0], p[1]], axis=1), jnp.concatenate([q[0], q[0]], axis=0)) for p, q in zip(low, t)
+    ]
+    v = [dot(p[0], q[1]) for p, q in zip(low, t)]
+    out = []
+    for x, y, w in zip(inverses, u, v):
+        y = y + w
+        pieces = []
+        for i, p in enumerate(odd):
+            pieces += [x[p.start - size : p.start], x[p] - y[size * i : size * (i + 1)]]
+        out.append(jnp.concatenate(pieces, axis=0))
+    return out
+
+
+def whole_inverses(inverses, corners):
+    parts = [split(x) for x in inverses]
+    t = [
+        split(dot(jnp.concatenate([e, e], axis=1), jnp.concatenate(parts[2 * b], axis=0)))
+        for b, e in enumerate(corners)
+    ]
+    u = [
+        dot(jnp.concatenate(parts[2 * b + 1], axis=1), jnp.concatenate([q[0], q[0]], axis=0)) for b, q in enumerate(t)
+    ]
+    v = [dot(parts[2 * b + 1][0], q[1]) for b, q in enumerate(t)]
+    gap = jnp.zeros((128, 128), BF16)
+    out = []
+    for b in range(len(corners)):
+        low = split(-(u[b] + v[b]))
+        out.append(
+            [
+                jnp.concatenate(
+                    [
+                        jnp.concatenate([parts[2 * b][i], gap], axis=1),
+                        jnp.concatenate([low[i], parts[2 * b + 1][i]], axis=1),
+                    ],
+                    axis=0,
+                )
+                for i in range(2)
+            ]
+        )
+    return out
 
 
 def kernel(
     slot_ref, target_ref, panel_hbm, rhs_hbm,
-    out_hbm, mean_ref,
-    panel_0, panel_1, state, diag_0, diag_1, work, inv_hi, inv_lo, solved, x_send, y_recv, z_send, z_recv, gathered, tgt,
-    load_sem, store_sem, send_sem, recv_sem, tgt_send, tgt_recv,
+    state, mean_ref,
+    panel_0, panel_1, low_0, diag_0, diag_1, work, inv_hi, inv_lo, solved, x_send, y_recv, z_send, z_recv, gathered, tgt,
+    load_sem, send_sem, recv_sem, tgt_send, tgt_recv,
 ):
     row, col = lax.axis_index("row"), lax.axis_index("col")
     y, z = row // NZ, row % NZ
@@ -140,12 +177,13 @@
         for t in range(blocks):
             load(panel_hbm.at[pl.ds(t * B, B), pl.ds(k * B, B)], panel[k].at[t], sem)
 
+    lower = [(b, a) for b in range(NCH) for a in range(b)]
     load_diag(0, 0)
     for t in range(blocks):
         load(rhs_hbm.at[pl.ds(t * B, B)], state.at[t], 1)
-    load_column(0, 2)
-    load_diag(1, 3)
-    load_column(1, 4)
+    for t in range(blocks):
+        for i, (b, a) in enumerate(lower):
+            load(panel_hbm.at[pl.ds(t * B + b * CH, CH), pl.ds(a * CH, CH)], low_0.at[t, i], 5)
 
     mine = [slot_ref[0] // blocks == row, slot_ref[1] // blocks == row]
     local = [slot_ref[0] % blocks, slot_ref[1] % blocks]
@@ -157,9 +195,9 @@
         found = join_inverses(
             lambda g: diag[k][local[k], pl.ds(128 * g, 128), pl.ds(128 * (g % 2), 128)]
         )
-        for b in range(NCH):
-            corner = diag[k][local[k], pl.ds(256 * b + 128, 128), pl.ds(0, 128)]
-            inv_hi[b], inv_lo[b] = whole_inverse(found, corner, b)
+        corners = [diag[k][local[k], pl.ds(CH * b + 128, 128), pl.ds(0, 128)] for b in range(NCH)]
+        for b, (hi, lo) in enumerate(whole_inverses(found, corners)):
+            inv_hi[b], inv_lo[b] = hi, lo
 
     def send(src, dst, k, c, stage, peer):
         pltpu.make_async_remote_copy(
@@ -172,7 +210,10 @@
         for b in range(NCH):
             part = work[pl.ds(b * CH, CH), :]
             for a in range(b):
-                tile = panel[k][local[k], pl.ds(b * CH, CH), pl.ds(a * CH, CH)]
+                if k == 0:
+                    tile = low_0[local[0], lower.index((b, a))]
+                else:
+                    tile = panel_1[local[1], pl.ds(b * CH, CH), pl.ds(a * CH, CH)]
                 part = part - (dot(tile, his[a]) + dot(tile, los[a]))
             hi, lo = split(part)
             ihi, ilo = inv_hi[b], inv_lo[b]
@@ -228,10 +269,13 @@
                 solved[k, pl.ds(c * CH + r, 16), pl.ds(128 * (i % 2), 128)] = gathered[k, c, j, i]
 
     wait_load(diag_0, 0)
+    load_diag(1, 3)
+    load_column(0, 2)
+    load_column(1, 4)
     invert(0)
     wait_load(state, 1)
     work[...] = state[local[0]]
-    wait_load(panel_0, 2)
+    wait_load(low_0, 5)
     solve(0)
     for c in range(NCH):
         reduce_y(0, c)
@@ -239,62 +283,55 @@
     invert(1)
     for c in range(NCH):
         reduce_z(0, c)
+    work[...] = state[local[1]]
     for c in range(NCH):
         gather_z(0, c)
+    wait_load(panel_0, 2)
     wait_load(panel_1, 4)
-    work[...] = state[local[1]]
     for c in range(NCH):
         gather_y(0, c)
         work[...] = work[...] - dot(panel_0[local[1], :, pl.ds(c * CH, CH)], solved[0, pl.ds(c * CH, CH), :])
     solve(1)
 
-    first_here = [slot_ref[0] == row * blocks + t for t in range(blocks)]
-    second_here = [slot_ref[1] == row * blocks + t for t in range(blocks)]
-
-    tile_rows = 256
-
-    def apply_first(t, i):
-        rows = pl.ds(pl.multiple_of(i * tile_rows, tile_rows), tile_rows)
-        term = dot(panel_0[t, rows, :], solved[0])
-        state[t, rows, :] = state[t, rows, :] - term
-
-    def apply_second(t, i):
-        rows = pl.ds(pl.multiple_of(i * tile_rows, tile_rows), tile_rows)
-        term = dot(panel_1[t, rows, :], solved[1])
-        value = state[t, rows, :] - term
-        value = jnp.where(second_here[t], solved[1, rows, :].astype(F32), value)
-        state[t, rows, :] = jnp.where(first_here[t], solved[0, rows, :].astype(F32), value)
-        pltpu.make_async_copy(
-            state.at[t, rows], out_hbm.at[pl.ds(t * B + pl.multiple_of(i * tile_rows, tile_rows), tile_rows)], store_sem
-        ).start()
+    def apply_first(t):
+        state[t] = state[t] - dot(panel_0[t], solved[0])
+
+    def apply_second(t, c):
+        part = pl.ds(c * CH, CH)
+        value = state[t] - dot(panel_1[t, :, part], solved[1, part, :])
+        if c == NCH - 1:
+            value = jnp.where(slot_ref[1] == row * blocks + t, solved[1].astype(F32), value)
+            value = jnp.where(slot_ref[0] == row * blocks + t, solved[0].astype(F32), value)
+        state[t] = value
+
+    def mean_terms(k):
+        mean = jnp.zeros((8, W), F32)
+        for d in range(NC):
+            rest = tgt[d]
+            for _ in range(3):
+                piece = rest.astype(BF16)
+                rest = rest - piece.astype(F32)
+                wide = jnp.concatenate([piece, jnp.zeros_like(piece)], axis=0)
+                mean = mean + dot(wide, solved[k, pl.ds(128 * d, 128), :])[0:8]
+        return mean[k : k + 1]
 
     for c in range(NCH):
         reduce_y(1, c)
-    for t in range(2):
-        lax.fori_loop(0, B // tile_rows, lambda i, _: apply_first(t, i), None)
+    apply_first(0)
+    apply_first(1)
     for c in range(NCH):
         reduce_z(1, c)
-    for t in range(2, 4):
-        lax.fori_loop(0, B // tile_rows, lambda i, _: apply_first(t, i), None)
+    apply_first(2)
+    apply_first(3)
     for c in range(NCH):
         gather_z(1, c)
     pltpu.make_async_copy(tgt.at[pl.ds(0, NC - 1)], tgt.at[pl.ds(0, NC - 1)], tgt_recv).wait()
+    mean = mean_terms(0)
     for c in range(NCH):
         gather_y(1, c)
-    for t in range(blocks):
-        lax.fori_loop(0, B // tile_rows, lambda i, _: apply_second(t, i), None)
-
-    mean = jnp.zeros((8, W), F32)
-    for d in range(NC):
-        rest = tgt[d]
-        for _ in range(3):
-            piece = rest.astype(BF16)
-            rest = rest - piece.astype(F32)
-            wide = jnp.concatenate([piece, jnp.zeros_like(piece)], axis=0)
-            for k in range(2):
-                found = dot(wide, solved[k, pl.ds(128 * d, 128), :])
-                mean = mean + jnp.where(iota((8, W), 0) == k, found[0:8], 0.0)
-    mean_ref[...] = mean[0:1] + mean[1:2]
+        for t in range(blocks):
+            apply_second(t, c)
+    mean_ref[...] = (mean + mean_terms(1)).reshape(W)
 
     for k in range(2):
         for c in range(NCH):
@@ -303,7 +340,6 @@
                 sent = ref.at[k, c, pl.ds(1, count)]
                 pltpu.make_async_copy(sent, sent, send_sem.at[k, c, stage]).wait()
     pltpu.make_async_copy(tgt.at[pl.ds(0, NC - 1)], tgt.at[pl.ds(0, NC - 1)], tgt_send).wait()
-    pltpu.make_async_copy(state, state, store_sem).wait()
 
 
 def per_device(panel, rhs, block_slot, target):
@@ -311,18 +347,18 @@
     piece = (NY, NZ, 16, 128)
     out, mean = pl.pallas_call(
         kernel,
-        out_shape=(jax.ShapeDtypeStruct((rows, width), F32), jax.ShapeDtypeStruct((1, width), F32)),
+        out_shape=(pltpu.VMEM((rows // B, B, width), F32), jax.ShapeDtypeStruct((width,), F32)),
         in_specs=[
             pl.BlockSpec(memory_space=pltpu.SMEM),
             pl.BlockSpec(memory_space=pltpu.VMEM),
             pl.BlockSpec(memory_space=pl.ANY),
             pl.BlockSpec(memory_space=pl.ANY),
         ],
-        out_specs=(pl.BlockSpec(memory_space=pl.ANY), pl.BlockSpec(memory_space=pltpu.VMEM)),
+        out_specs=(pl.BlockSpec(memory_space=pltpu.VMEM), pl.BlockSpec(memory_space=pltpu.VMEM)),
         scratch_shapes=[
             pltpu.VMEM((4, B, B), BF16),
             pltpu.VMEM((4, B, B), BF16),
-            pltpu.VMEM((4, B, W), F32),
+            pltpu.VMEM((4, 6, CH, CH), BF16),
             pltpu.VMEM((4, B, CH), BF16),
             pltpu.VMEM((4, B, CH), BF16),
             pltpu.VMEM((B, W), F32),
@@ -335,8 +371,7 @@
             pltpu.VMEM((2, NCH) + piece[1:], BF16),
             pltpu.VMEM((2, NCH) + piece, BF16),
             pltpu.VMEM((NC, 8, 128), F32),
-            pltpu.SemaphoreType.DMA((5,)),
-            pltpu.SemaphoreType.DMA,
+            pltpu.SemaphoreType.DMA((6,)),
             pltpu.SemaphoreType.DMA((2, NCH, 4)),
             pltpu.SemaphoreType.DMA((2, NCH, 4)),
             pltpu.SemaphoreType.DMA,
@@ -347,7 +382,7 @@
         ),
         name="substitute",
     )(block_slot, target, panel, rhs)
-    return out, mean.reshape(width)
+    return out.reshape(rows, width), mean
 
 
 def solution(mesh):

time: 72.3 us -> 58.3 us (0.81)
  Pallas kernels: 66.5 us -> 54.9 us
  local copies, waits for them, and re-layouts: 5.04 us -> 2.58 us
    pallas_call x1, Pallas kernels: 66.5 us -> 54.9 us  [per_device(): pl.pallas_call(kernel, out_shape=(pltpu.VMEM((rows // B, B, width), F32),...]
    unnamed x4, local copies, waits for them, and re-layouts: 5.04 us -> 2.58 us
where the time goes in v2:
time: 58.3 us; the launch traced here: 58.2 us
  Pallas kernels  54.9 us (94%)
  local copies, waits for them, and re-layouts  2.58 us (4%)
  between operations  0.65 us (1%)
    pallas_call x1, Pallas kernels, per_device(): pl.pallas_call(kernel, out_shape=(pltpu.VMEM((rows // B, B, width), F32),...  54.9 us
    unnamed x4, local copies, waits for them, and re-layouts  2.58 us

profile of v2, /device:TPU:6, one launch (start us, length us, event | category | flops | bytes accessed | tf_op | source)
XLA Modules:
  0.0 58.2 jit_solution(16095331640397845063)
XLA Ops:
  0.6 54.9 %substitute.1 = (f32[4,1024,256]{2,1,0:T(8,128)S(1)}, f32[256]{0:T(256)}) custom-call(s32[128]{0:T(128)} %slot_ref.1, f32[2,128]{1,0:T(2,128)} %target_ref.1, bf16[4096,2048]{1,0:T(8,128)(2,1)} %panel_hbm.1, f32[4096,256]{1,0:T(8,128)} %rhs_hbm.1), custom_call_target="tpu_custom_call" | custom-call | tf_op jit(solution)/shard_map/substitute/pallas_call | solution.py:348
  55.6 0.0 copy-start
  55.6 2.0 %copy.8 = f32[4096,256]{1,0:T(8,128)} copy(f32[4096,256]{1,0:T(8,128)S(1)} %bitcast.1) | data formatting | bytes 8388608
  57.6 0.0 copy-done
  57.6 0.6 copy.9
Async XLA Ops:
  55.6 2.0 %copy-start = (f32[256]{0:T(256)S(1)}, f32[256]{0:T(256)}, u32[]{:S(2)}) copy-start(f32[256]{0:T(256)} %get-tuple-element.11) | copy-start | bytes 3076

commit v3 on v2

--- a/solution.py
+++ b/solution.py
@@ -13,6 +13,7 @@
 CH = 256
 NCH = B // CH
 BASE = 16
+PIECE = CH // 8
 F32, BF16 = jnp.float32, jnp.bfloat16
 MESH = pl.DeviceIdType.MESH
 
@@ -142,18 +143,33 @@
 def kernel(
     slot_ref, target_ref, panel_hbm, rhs_hbm,
     state, mean_ref,
-    panel_0, panel_1, low_0, diag_0, diag_1, work, inv_hi, inv_lo, solved, x_send, y_recv, z_send, z_recv, gathered, tgt,
+    panel_0, panel_1, low_0, diag_0, diag_1, work, inv_hi, inv_lo, solved, x_send, near_recv, z_send, z_recv, tgt,
     load_sem, send_sem, recv_sem, tgt_send, tgt_recv,
 ):
     row, col = lax.axis_index("row"), lax.axis_index("col")
     y, z = row // NZ, row % NZ
-    y_peers = [(lax.rem(y + d, NY) * NZ + z, col) for d in range(1, NY)]
-    z_peers = [(y * NZ + lax.rem(z + d, NZ), col) for d in range(1, NZ)]
+
+    def half(c):
+        return lax.rem(z + c % 2, 2)
+
+    def near(c, dy, flip):
+        step = flip * (1 - 2 * half(c))
+        return (lax.rem(y + dy, NY) * NZ + lax.rem(z + step + NZ, NZ), col)
+
+    def near_rows(c, dy, flip):
+        slot = lax.rem(y + dy, NY) * 2 + half(c) + flip * (1 - 2 * half(c))
+        return pl.ds(pl.multiple_of(c * CH + slot * PIECE, PIECE), PIECE)
+
+    around = [(2, 1), (1, 1), (3, 1), (2, 0), (1, 0), (3, 0), (0, 1)]
+    along = [4, 2, 6]
+    z_peers = [(y * NZ + lax.rem(z + d, NZ), col) for d in along]
     c_peers = [(row, lax.rem(col + d, NC)) for d in range(1, NC)]
     tgt[...] = jnp.zeros_like(tgt)
     tgt[col, 0:2, :] = target_ref[...]
     barrier = pltpu.get_barrier_semaphore()
-    for peer in y_peers + z_peers + c_peers:
+    near_peers = [near(0, dy, flip) for dy, flip in around] + [near(1, dy, flip) for dy, flip in around if flip]
+    peers = near_peers + z_peers + c_peers
+    for peer in peers:
         pl.semaphore_signal(barrier, inc=1, device_id=peer, device_id_type=MESH)
 
     def load(src, dst, k):
@@ -222,51 +238,40 @@
             his.append(hi)
             los.append(lo)
             masked = jnp.where(mine[k], x, 0.0).astype(BF16)
-            for j in range(NY):
-                for i in range(NZ):
-                    r = 64 * j + 16 * (i // 2)
-                    x_send[k, b, j, i] = masked[r : r + 16, 128 * (i % 2) : 128 * (i % 2 + 1)]
+            x_send[k, pl.ds(b * CH, CH), :] = masked
             if k == 0 and b == 0:
-                pl.semaphore_wait(barrier, NY + NZ + NC - 3)
+                pl.semaphore_wait(barrier, len(peers))
                 for peer in c_peers:
                     pltpu.make_async_remote_copy(
                         src_ref=tgt.at[col], dst_ref=tgt.at[col], send_sem=tgt_send, recv_sem=tgt_recv,
                         device_id=peer, device_id_type=MESH,
                     ).start()
-            for d in range(1, NY):
-                send(x_send.at[k, b, lax.rem(y + d, NY)], y_recv.at[k, b, d], k, b, 0, y_peers[d - 1])
+            for dy, flip in around:
+                send(x_send.at[k, near_rows(b, dy, flip)], near_recv.at[k, b, dy * 2 + flip], k, b, 0, near(b, dy, flip))
 
     def arrived(ref, k, c, stage):
         pltpu.make_async_copy(ref, ref, recv_sem.at[k, c, stage]).wait()
 
-    def reduce_y(k, c):
-        arrived(y_recv.at[k, c, pl.ds(1, NY - 1)], k, c, 0)
-        z_send[k, c] = (x_send[k, c, y] + y_recv[k, c, 1]) + (y_recv[k, c, 2] + y_recv[k, c, 3])
-        for d in range(1, NZ):
-            send(z_send.at[k, c, lax.rem(z + d, NZ)], z_recv.at[k, c, d], k, c, 1, z_peers[d - 1])
-
-    def reduce_z(k, c):
-        arrived(z_recv.at[k, c, pl.ds(1, NZ - 1)], k, c, 1)
-        total = z_send[k, c, z]
-        for d in range(1, NZ):
-            total = total + z_recv[k, c, d]
-        gathered[k, c, y, z] = total
-        piece = gathered.at[k, c, y, z]
-        for d in range(1, NZ):
-            send(piece, piece, k, c, 2, z_peers[d - 1])
-
-    def gather_z(k, c):
-        arrived(z_recv.at[k, c, pl.ds(1, NZ - 1)], k, c, 2)
-        piece = gathered.at[k, c, y]
-        for d in range(1, NY):
-            send(piece, piece, k, c, 3, y_peers[d - 1])
-
-    def gather_y(k, c):
-        arrived(y_recv.at[k, c, pl.ds(1, NY - 1)], k, c, 3)
-        for j in range(NY):
-            for i in range(NZ):
-                r = 64 * j + 16 * (i // 2)
-                solved[k, pl.ds(c * CH + r, 16), pl.ds(128 * (i % 2), 128)] = gathered[k, c, j, i]
+    def reduce_near(k, c):
+        arrived(near_recv.at[k, c, pl.ds(1, 7)], k, c, 0)
+        total = x_send[k, near_rows(c, 0, 0), :]
+        for d in range(1, 8):
+            total = total + near_recv[k, c, d]
+        z_send[k, c] = total
+        for d, peer in zip(along, z_peers):
+            send(z_send.at[k, c], z_recv.at[k, c, d // 2], k, c, 1, peer)
+
+    def reduce_along(k, c):
+        arrived(z_recv.at[k, c, pl.ds(1, 3)], k, c, 1)
+        total = (z_send[k, c] + z_recv[k, c, 1]) + (z_recv[k, c, 2] + z_recv[k, c, 3])
+        mine_here = near_rows(c, 0, 0)
+        solved[k, mine_here, :] = total
+        piece = solved.at[k, mine_here]
+        for dy, flip in around:
+            send(piece, piece, k, c, 2, near(c, dy, flip))
+
+    def gather(k, c):
+        arrived(near_recv.at[k, c, pl.ds(1, 7)], k, c, 2)
 
     wait_load(diag_0, 0)
     load_diag(1, 3)
@@ -278,18 +283,16 @@
     wait_load(low_0, 5)
     solve(0)
     for c in range(NCH):
-        reduce_y(0, c)
+        reduce_near(0, c)
     wait_load(diag_1, 3)
     invert(1)
     for c in range(NCH):
-        reduce_z(0, c)
+        reduce_along(0, c)
     work[...] = state[local[1]]
-    for c in range(NCH):
-        gather_z(0, c)
     wait_load(panel_0, 2)
     wait_load(panel_1, 4)
     for c in range(NCH):
-        gather_y(0, c)
+        gather(0, c)
         work[...] = work[...] - dot(panel_0[local[1], :, pl.ds(c * CH, CH)], solved[0, pl.ds(c * CH, CH), :])
     solve(1)
 
@@ -304,47 +307,45 @@
             value = jnp.where(slot_ref[0] == row * blocks + t, solved[0].astype(F32), value)
         state[t] = value
 
-    def mean_terms(k):
-        mean = jnp.zeros((8, W), F32)
-        for d in range(NC):
-            rest = tgt[d]
-            for _ in range(3):
-                piece = rest.astype(BF16)
-                rest = rest - piece.astype(F32)
-                wide = jnp.concatenate([piece, jnp.zeros_like(piece)], axis=0)
-                mean = mean + dot(wide, solved[k, pl.ds(128 * d, 128), :])[0:8]
-        return mean[k : k + 1]
-
-    for c in range(NCH):
-        reduce_y(1, c)
+    def mean_weights():
+        rest = jnp.concatenate([tgt[d] for d in range(NC)], axis=1)
+        parts = []
+        for _ in range(3):
+            parts.append(rest.astype(BF16).astype(F32))
+            rest = rest - parts[-1]
+        return jnp.concatenate(parts + [jnp.zeros_like(rest)], axis=0).astype(BF16)
+
+    def mean_terms(weights, k):
+        found = dot(weights, solved[k])
+        return found[k : k + 1] + found[8 + k : 9 + k] + found[16 + k : 17 + k]
+
     apply_first(0)
+    for c in range(NCH):
+        reduce_near(1, c)
     apply_first(1)
-    for c in range(NCH):
-        reduce_z(1, c)
     apply_first(2)
+    for c in range(NCH):
+        reduce_along(1, c)
     apply_first(3)
-    for c in range(NCH):
-        gather_z(1, c)
     pltpu.make_async_copy(tgt.at[pl.ds(0, NC - 1)], tgt.at[pl.ds(0, NC - 1)], tgt_recv).wait()
-    mean = mean_terms(0)
-    for c in range(NCH):
-        gather_y(1, c)
+    weights = mean_weights()
+    mean = mean_terms(weights, 0)
+    for c in range(NCH):
+        gather(1, c)
         for t in range(blocks):
             apply_second(t, c)
-    mean_ref[...] = (mean + mean_terms(1)).reshape(W)
+    mean_ref[...] = (mean + mean_terms(weights, 1)).reshape(W)
 
     for k in range(2):
         for c in range(NCH):
-            for stage, ref in enumerate((y_recv, z_recv, z_recv, y_recv)):
-                count = (NY if stage in (0, 3) else NZ) - 1
-                sent = ref.at[k, c, pl.ds(1, count)]
+            for stage, sent in enumerate((near_recv.at[k, c, pl.ds(1, 7)], z_recv.at[k, c, pl.ds(1, 3)], near_recv.at[k, c, pl.ds(1, 7)])):
                 pltpu.make_async_copy(sent, sent, send_sem.at[k, c, stage]).wait()
     pltpu.make_async_copy(tgt.at[pl.ds(0, NC - 1)], tgt.at[pl.ds(0, NC - 1)], tgt_send).wait()
 
 
 def per_device(panel, rhs, block_slot, target):
     rows, width = rhs.shape
-    piece = (NY, NZ, 16, 128)
+    piece = (PIECE, W)
     out, mean = pl.pallas_call(
         kernel,
         out_shape=(pltpu.VMEM((rows // B, B, width), F32), jax.ShapeDtypeStruct((width,), F32)),
@@ -365,15 +366,14 @@
             pltpu.VMEM((NCH, CH, CH), BF16),
             pltpu.VMEM((NCH, CH, CH), BF16),
             pltpu.VMEM((2, B, W), BF16),
+            pltpu.VMEM((2, B, W), BF16),
+            pltpu.VMEM((2, NCH, 8) + piece, BF16),
             pltpu.VMEM((2, NCH) + piece, BF16),
-            pltpu.VMEM((2, NCH) + piece, BF16),
-            pltpu.VMEM((2, NCH) + piece[1:], BF16),
-            pltpu.VMEM((2, NCH) + piece[1:], BF16),
-            pltpu.VMEM((2, NCH) + piece, BF16),
+            pltpu.VMEM((2, NCH, 4) + piece, BF16),
             pltpu.VMEM((NC, 8, 128), F32),
             pltpu.SemaphoreType.DMA((6,)),
-            pltpu.SemaphoreType.DMA((2, NCH, 4)),
-            pltpu.SemaphoreType.DMA((2, NCH, 4)),
+            pltpu.SemaphoreType.DMA((2, NCH, 3)),
+            pltpu.SemaphoreType.DMA((2, NCH, 3)),
             pltpu.SemaphoreType.DMA,
             pltpu.SemaphoreType.DMA,
         ],

time: 58.3 us -> 55.2 us (0.947)
  Pallas kernels: 54.9 us -> 51.9 us
    pallas_call x1, Pallas kernels: 54.9 us -> 51.9 us  [per_device(): pl.pallas_call(kernel, out_shape=(pltpu.VMEM((rows // B, B, width), F32),...]
where the time goes in v3:
time: 55.2 us; the launch traced here: 55.1 us
  Pallas kernels  51.9 us (94%)
  local copies, waits for them, and re-layouts  2.58 us (5%)
  between operations  0.65 us (1%)
    pallas_call x1, Pallas kernels, per_device(): pl.pallas_call(kernel, out_shape=(pltpu.VMEM((rows // B, B, width), F32),...  51.9 us
    unnamed x4, local copies, waits for them, and re-layouts  2.58 us

profile of v3, /device:TPU:6, one launch (start us, length us, event | category | flops | bytes accessed | tf_op | source)
XLA Modules:
  0.0 55.1 jit_solution(6577885904053099983)
XLA Ops:
  0.6 51.9 %substitute.1 = (f32[4,1024,256]{2,1,0:T(8,128)S(1)}, f32[256]{0:T(256)}) custom-call(s32[128]{0:T(128)} %slot_ref.1, f32[2,128]{1,0:T(2,128)} %target_ref.1, bf16[4096,2048]{1,0:T(8,128)(2,1)} %panel_hbm.1, f32[4096,256]{1,0:T(8,128)} %rhs_hbm.1), custom_call_target="tpu_custom_call" | custom-call | tf_op jit(solution)/shard_map/substitute/pallas_call | solution.py:349
  52.5 0.0 copy-start
  52.5 2.0 %copy.8 = f32[4096,256]{1,0:T(8,128)} copy(f32[4096,256]{1,0:T(8,128)S(1)} %bitcast.1) | data formatting | bytes 8388608
  54.5 0.0 copy-done
  54.5 0.6 %copy.9 = f32[256]{0:T(256)} copy(f32[256]{0:T(256)S(1)} %copy-done) | data formatting | bytes 2048
Async XLA Ops:
  52.5 2.0 %copy-start = (f32[256]{0:T(256)S(1)}, f32[256]{0:T(256)}, u32[]{:S(2)}) copy-start(f32[256]{0:T(256)} %get-tuple-element.11) | copy-start | bytes 3076

commit v4 on v3

v4 whole, which is shorter than its diff:
```python
import functools

import jax
import jax.numpy as jnp
from jax import lax
from jax.experimental import pallas as pl
from jax.experimental.pallas import tpu as pltpu
from jax.sharding import PartitionSpec as P

B = 1024
W = 256
NY, NZ, NC = 4, 8, 8
CH = 256
NCH = B // CH
BASE = 16
PIECE = CH // 8
PARTS = 10
PARTS_M, PARTS_0, PARTS_1 = [0, 1], [2, 3, 4, 5], [6, 7, 8, 9]
F32, BF16 = jnp.float32, jnp.bfloat16
MESH = pl.DeviceIdType.MESH


def dot(a, b):
    return jnp.dot(a, b, preferred_element_type=F32)


def split(x):
    hi = x.astype(BF16)
    return hi, (x - hi.astype(F32)).astype(BF16)


def iota(shape, dim):
    return lax.broadcasted_iota(jnp.int32, shape, dim)


def spread_matrix():
    shape = (128, BASE * 128)
    lane = iota(shape, 1)
    return jnp.where(iota(shape, 0) == (lane % 128) // BASE * BASE + lane // 128, 1.0, 0.0).astype(BF16)


def invert_small(blocks, spread):
    groups = len(blocks)
    lane = iota((BASE, 128), 1)
    packed = []
    for block in blocks:
        wide = block.astype(F32)
        acc = jnp.zeros((BASE, 128), F32)
        for b in range(128 // BASE):
            acc = jnp.where(lane // BASE == b, wide[BASE * b : BASE * (b + 1)], acc)
        packed.append(acc)
    packed = jnp.concatenate(packed, axis=0).astype(BF16)
    factors = dot(packed, spread)
    part = [factors[:, 128 * j : 128 * (j + 1)].reshape(groups, BASE, 128) for j in range(BASE)]
    row = iota((groups, BASE, 128), 1)
    diag = part[0]
    for j in range(1, BASE):
        diag = jnp.where(row == j, part[j], diag)
    scale = 1.0 / diag
    x = jnp.where(iota((groups, BASE, 128), 2) % BASE == row, scale, 0.0)
    for j in range(BASE - 1):
        factor = jnp.where(row > j, part[j] * scale, 0.0)
        x = x - factor * x[:, j : j + 1, :]
    return [x[g] for g in range(groups)]


def join_inverses(diag_block):
    groups = B // 128
    spread = spread_matrix()
    blocks = [diag_block(g) for g in range(groups)]
    small = invert_small(blocks, spread)
    r, c = iota((128, 128), 0), iota((128, 128), 1)
    inverses = []
    for g in range(groups):
        tiled = jnp.concatenate([small[g]] * (128 // BASE), axis=0)
        inverses.append(jnp.where(r // BASE == c // BASE, tiled, 0.0))
    size = BASE
    while size < 128:
        odd = [slice(i, i + size) for i in range(size, 128, 2 * size)]
        mask = (c // size == r // size - 1) & ((r // size) % 2 == 1)
        off = [rows_of(jnp.where(mask, block, jnp.zeros_like(block)), odd) for block in blocks]
        inverses = joined(inverses, off, odd)
        size *= 2
    return inverses


def rows_of(x, parts):
    return jnp.concatenate([x[p] for p in parts], axis=0)


def joined(inverses, off, odd):
    size = odd[0].stop - odd[0].start
    parts = [split(x) for x in inverses]
    low = [(rows_of(hi, odd), rows_of(lo, odd)) for hi, lo in parts]
    t = [split(dot(jnp.concatenate([e, e], axis=1), jnp.concatenate(p, axis=0))) for e, p in zip(off, parts)]

    def spread_rows(x):
        gap = jnp.zeros((size, x.shape[1]), x.dtype)
        return jnp.concatenate([v for i in range(len(odd)) for v in (gap, x[size * i : size * (i + 1)])], axis=0)

    t = [(spread_rows(hi), spread_rows(lo)) for hi, lo in t]
    u = [
        dot(jnp.concatenate([p[0], p[1]], axis=1), jnp.concatenate([q[0], q[0]], axis=0)) for p, q in zip(low, t)
    ]
    v = [dot(p[0], q[1]) for p, q in zip(low, t)]
    out = []
    for x, y, w in zip(inverses, u, v):
        y = y + w
        pieces = []
        for i, p in enumerate(odd):
            pieces += [x[p.start - size : p.start], x[p] - y[size * i : size * (i + 1)]]
        out.append(jnp.concatenate(pieces, axis=0))
    return out


def whole_inverses(inverses, corners):
    parts = [split(x) for x in inverses]
    t = [
        split(dot(jnp.concatenate([e, e], axis=1), jnp.concatenate(parts[2 * b], axis=0)))
        for b, e in enumerate(corners)
    ]
    u = [
        dot(jnp.concatenate(parts[2 * b + 1], axis=1), jnp.concatenate([q[0], q[0]], axis=0)) for b, q in enumerate(t)
    ]
    v = [dot(parts[2 * b + 1][0], q[1]) for b, q in enumerate(t)]
    gap = jnp.zeros((128, 128), BF16)
    out = []
    for b in range(len(corners)):
        low = split(-(u[b] + v[b]))
        out.append(
            [
                jnp.concatenate(
                    [
                        jnp.concatenate([parts[2 * b][i], gap], axis=1),
                        jnp.concatenate([low[i], parts[2 * b + 1][i]], axis=1),
                    ],
                    axis=0,
                )
                for i in range(2)
            ]
        )
    return out


def prepare(
    slot_ref, panel_hbm, rhs_hbm, out, diag, low, right, cross, inv_hi, inv_lo, load_sem,
):
    row, col = lax.axis_index("row"), lax.axis_index("col")
    blocks = 4
    lower = [(b, a) for b in range(NCH) for a in range(b)]

    def load(src, dst, k):
        pltpu.make_async_copy(src, dst, load_sem.at[k]).start()

    def wait_load(ref, k):
        pltpu.make_async_copy(ref, ref, load_sem.at[k]).wait()

    def job(k):
        start = (slot_ref[k] % blocks) * B
        at = lambda b: pl.ds(pl.multiple_of(start + b * CH, CH), CH)
        whole = pl.ds(pl.multiple_of(start, B), B)
        for b in range(NCH):
            load(panel_hbm.at[at(b), pl.ds(k * B + b * CH, CH)], diag.at[pl.ds(b * CH, CH)], 0)
        load(rhs_hbm.at[whole], right, 1)
        if k == 1:
            load(panel_hbm.at[whole, pl.ds(pl.multiple_of(col * 128, 128), 128)], cross, 2)
        for i, (b, a) in enumerate(lower):
            load(panel_hbm.at[at(b), pl.ds(k * B + a * CH, CH)], low.at[i], 3)
        wait_load(diag, 0)
        found = join_inverses(lambda g: diag[pl.ds(128 * g, 128), pl.ds(128 * (g % 2), 128)])
        corners = [diag[pl.ds(CH * b + 128, 128), pl.ds(0, 128)] for b in range(NCH)]
        for b, (hi, lo) in enumerate(whole_inverses(found, corners)):
            inv_hi[b], inv_lo[b] = hi, lo
        wait_load(right, 1)
        if k == 1:
            wait_load(cross, 2)
        wait_load(low, 3)
        his, los = [], []
        for b in range(NCH):
            rows = pl.ds(b * CH, CH)
            part = right[rows, :]
            if k == 1:
                part = jnp.concatenate([part, cross[rows, :].astype(F32)], axis=1)
            for a in range(b):
                tile = low[lower.index((b, a))]
                part = part - (dot(tile, his[a]) + dot(tile, los[a]))
            hi, lo = split(part)
            ihi, ilo = inv_hi[b], inv_lo[b]
            x = dot(ihi, hi) + (dot(ihi, lo) + dot(ilo, hi))
            hi, lo = split(x)
            his.append(hi)
            los.append(lo)
            out[pl.ds((PARTS_0[b] if k == 0 else PARTS_1[b]) * CH, CH), :] = hi[:, :W]
            if k == 1:
                out[pl.ds(PARTS_M[b // 2] * CH, CH), pl.ds(128 * (b % 2), 128)] = hi[:, W:]

    spans = [[(PARTS_0[0], NCH)], [(PARTS_M[0], 2), (PARTS_1[0], NCH)]]
    for k in range(2):
        mine = slot_ref[k] // blocks == row
        pl.when(mine)(functools.partial(job, k))

        @pl.when(jnp.logical_not(mine))
        def _():
            for first, count in spans[k]:
                out[pl.ds(first * CH, count * CH), :] = jnp.zeros((count * CH, W), BF16)


def kernel(
    slot_ref, target_ref, x_send, panel_hbm, rhs_hbm,
    state, mean_ref,
    panel_0, panel_1, second, second_wide,
    near_recv, z_send, z_recv, got, middle, tgt,
    load_sem, send_sem, recv_sem, x_sem, core_sem, pass_sem, tgt_sem,
):
    row, col = lax.axis_index("row"), lax.axis_index("col")
    y, z = row // NZ, row % NZ

    def half(q):
        return lax.rem(z + q % 2, 2)

    def near(q, dy, flip):
        step = flip * (1 - 2 * half(q))
        return (lax.rem(y + dy, NY) * NZ + lax.rem(z + step + NZ, NZ), col)

    def near_rows(q, dy, flip):
        slot = lax.rem(y + dy, NY) * 2 + half(q) + flip * (1 - 2 * half(q))
        return pl.ds(pl.multiple_of(q * CH + slot * PIECE, PIECE), PIECE)

    around = [(2, 1), (1, 1), (3, 1), (2, 0), (1, 0), (3, 0), (0, 1)]
    along = [4, 2, 6]
    z_peers = [(y * NZ + lax.rem(z + d, NZ), col) for d in along]
    c_peers = [(row, lax.rem(col + d, NC)) for d in range(1, NC)]
    x_cols = [lax.rem(col + d, NC) for d in (4, 2, 6)]
    sibling = (row, col + 1 - 2 * lax.rem(col, 2))
    tgt[...] = jnp.zeros_like(tgt)
    tgt[col, 0:2, :] = target_ref[...]
    barrier = pltpu.get_barrier_semaphore()
    near_peers = [near(0, dy, flip) for dy, flip in around] + [near(1, dy, flip) for dy, flip in around if flip]
    peers = near_peers + z_peers + c_peers
    for peer in peers:
        pl.semaphore_signal(barrier, inc=1, device_id=peer, device_id_type=MESH)

    blocks = 4
    panel = [panel_0, panel_1]

    def load(src, dst, k):
        pltpu.make_async_copy(src, dst, load_sem.at[k]).start()

    def load_column(k):
        for t in range(blocks):
            load(panel_hbm.at[pl.ds(t * B, B), pl.ds(k * B, B)], panel[k].at[t], k)

    def wait_load(ref, k):
        pltpu.make_async_copy(ref, ref, load_sem.at[k]).wait()

    def rows_of_part(q):
        return pl.ds(q * CH, CH)

    def send(src, dst, q, stage, peer):
        pltpu.make_async_remote_copy(
            src_ref=src, dst_ref=dst, send_sem=send_sem.at[q, stage], recv_sem=recv_sem.at[q, stage],
            device_id=peer, device_id_type=MESH,
        ).start()

    def arrived(ref, sem):
        pltpu.make_async_copy(ref, ref, sem).wait()

    def spread(q):
        for dy, flip in around:
            send(x_send.at[near_rows(q, dy, flip)], near_recv.at[q, dy * 2 + flip], q, 0, near(q, dy, flip))

    def reduce_near(q):
        arrived(near_recv.at[q, pl.ds(1, 7)], recv_sem.at[q, 0])
        total = x_send[near_rows(q, 0, 0), :]
        for d in range(1, 8):
            total = total + near_recv[q, d]
        z_send[q] = total
        for d, peer in zip(along, z_peers):
            send(z_send.at[q], z_recv.at[q, d // 2], q, 1, peer)

    def reduce_along(q):
        arrived(z_recv.at[q, pl.ds(1, 3)], recv_sem.at[q, 1])
        mine_here = near_rows(q, 0, 0)
        got[mine_here, :] = (z_send[q] + z_recv[q, 1]) + (z_recv[q, 2] + z_recv[q, 3])
        piece = got.at[mine_here]
        for dy, flip in around:
            send(piece, piece, q, 2, near(q, dy, flip))

    def gather(q):
        arrived(near_recv.at[q, pl.ds(1, 7)], recv_sem.at[q, 2])

    def across(src, dst, sem, q, peer):
        pltpu.make_async_remote_copy(
            src_ref=src, dst_ref=dst, send_sem=sem.at[0, q], recv_sem=sem.at[1, q],
            device_id=peer, device_id_type=MESH,
        ).start()

    def middle_out(q):
        rows = rows_of_part(q)
        for other in x_cols:
            across(got.at[rows], middle.at[col, rows], x_sem, q, (row, other))
        across(got.at[rows], middle.at[col, rows], core_sem, q, sibling)
        middle[col, rows, :] = got[rows, :]

    def middle_on(q):
        rows = rows_of_part(q)
        arrived(middle.at[pl.ds(0, 3), rows], x_sem.at[1, q])
        for other in x_cols:
            across(middle.at[other, rows], middle.at[other, rows], pass_sem, q, sibling)

    def middle_in(q):
        rows = rows_of_part(q)
        arrived(middle.at[0, rows], core_sem.at[1, q])
        arrived(middle.at[pl.ds(0, 3), rows], pass_sem.at[1, q])

    parts_m, parts_0, parts_1 = PARTS_M, PARTS_0, PARTS_1
    pl.semaphore_wait(barrier, len(peers))
    for q in parts_m + parts_0 + parts_1:
        spread(q)
    for t in range(blocks):
        load(rhs_hbm.at[pl.ds(t * B, B)], state.at[t], 2)
    load_column(0)
    load_column(1)
    for peer in c_peers:
        pltpu.make_async_remote_copy(
            src_ref=tgt.at[col], dst_ref=tgt.at[col], send_sem=tgt_sem.at[0], recv_sem=tgt_sem.at[1],
            device_id=peer, device_id_type=MESH,
        ).start()
    for q in parts_m + parts_0:
        reduce_near(q)
    for q in parts_m:
        reduce_along(q)
    for q in parts_1[:2]:
        reduce_near(q)
    for q in parts_m:
        gather(q)
        middle_out(q)
    for q in parts_1[2:]:
        reduce_near(q)
    for q in parts_0 + parts_1:
        reduce_along(q)
    for q in parts_m:
        middle_on(q)
    wait_load(state, 2)
    wait_load(panel_0, 0)
    wait_load(panel_1, 1)
    for q in parts_0:
        gather(q)

    first_rows = pl.ds(parts_0[0] * CH, B)

    def apply_first(t):
        state[t] = state[t] - dot(panel_0[t], got[first_rows, :])

    def apply_second(t):
        value = state[t] - dot(panel_1[t], second[...])
        value = jnp.where(slot_ref[1] == row * blocks + t, second_wide[...], value)
        value = jnp.where(slot_ref[0] == row * blocks + t, got[first_rows, :].astype(F32), value)
        state[t] = value

    def mean_weights():
        rest = jnp.concatenate([tgt[d] for d in range(NC)], axis=1)
        parts = []
        for _ in range(3):
            parts.append(rest.astype(BF16).astype(F32))
            rest = rest - parts[-1]
        return jnp.concatenate(parts + [jnp.zeros_like(rest)], axis=0).astype(BF16)

    def mean_terms(found, k):
        return found[k : k + 1] + found[8 + k : 9 + k] + found[16 + k : 17 + k]

    for t in range(blocks):
        apply_first(t)
    arrived(tgt.at[pl.ds(0, NC - 1)], tgt_sem.at[1])
    weights = mean_weights()
    mean = mean_terms(dot(weights, got[first_rows, :]), 0)
    for q in parts_1:
        gather(q)
    for q in parts_m:
        middle_in(q)
    for b in range(NCH):
        rows = rows_of_part(b)
        wide = jnp.concatenate(
            [middle[j, rows_of_part(b // 2), pl.ds(128 * (b % 2), 128)] for j in range(NC)], axis=1
        )
        x = got[rows_of_part(parts_1[b]), :].astype(F32) - dot(wide, got[first_rows, :])
        second_wide[rows, :] = x
        second[rows, :] = x.astype(BF16)
    for t in range(blocks):
        apply_second(t)
    hi, lo = split(second_wide[...])
    mean_ref[...] = (mean + mean_terms(dot(weights, hi) + dot(weights, lo), 1)).reshape(W)

    for q in range(PARTS):
        for stage, sent in enumerate((near_recv.at[q, pl.ds(1, 7)], z_recv.at[q, pl.ds(1, 3)], near_recv.at[q, pl.ds(1, 7)])):
            arrived(sent, send_sem.at[q, stage])
    for q in parts_m:
        rows = rows_of_part(q)
        arrived(middle.at[pl.ds(0, 3), rows], x_sem.at[0, q])
        arrived(middle.at[0, rows], core_sem.at[0, q])
        arrived(middle.at[pl.ds(0, 3), rows], pass_sem.at[0, q])
    arrived(tgt.at[pl.ds(0, NC - 1)], tgt_sem.at[0])


def per_device(panel, rhs, block_slot, target):
    rows, width = rhs.shape
    piece = (PIECE, W)
    ready = pl.pallas_call(
        prepare,
        out_shape=pltpu.VMEM((PARTS * CH, W), BF16),
        in_specs=[
            pl.BlockSpec(memory_space=pltpu.SMEM),
            pl.BlockSpec(memory_space=pl.ANY),
            pl.BlockSpec(memory_space=pl.ANY),
        ],
        out_specs=pl.BlockSpec(memory_space=pltpu.VMEM),
        scratch_shapes=[
            pltpu.VMEM((B, CH), BF16),
            pltpu.VMEM((6, CH, CH), BF16),
            pltpu.VMEM((B, W), F32),
            pltpu.VMEM((B, 128), BF16),
            pltpu.VMEM((NCH, CH, CH), BF16),
            pltpu.VMEM((NCH, CH, CH), BF16),
            pltpu.SemaphoreType.DMA((4,)),
        ],
        compiler_params=pltpu.CompilerParams(vmem_limit_bytes=58 * 2**20),
        name="prepare",
    )(block_slot, panel, rhs)
    ready = pltpu.with_memory_space_constraint(ready, pltpu.VMEM)
    out, mean = pl.pallas_call(
        kernel,
        out_shape=(pltpu.VMEM((rows // B, B, width), F32), jax.ShapeDtypeStruct((width,), F32)),
        in_specs=[
            pl.BlockSpec(memory_space=pltpu.SMEM),
            pl.BlockSpec(memory_space=pltpu.VMEM),
            pl.BlockSpec(memory_space=pltpu.VMEM),
            pl.BlockSpec(memory_space=pl.ANY),
            pl.BlockSpec(memory_space=pl.ANY),
        ],
        out_specs=(pl.BlockSpec(memory_space=pltpu.VMEM), pl.BlockSpec(memory_space=pltpu.VMEM)),
        scratch_shapes=[
            pltpu.VMEM((4, B, B), BF16),
            pltpu.VMEM((4, B, B), BF16),
            pltpu.VMEM((B, W), BF16),
            pltpu.VMEM((B, W), F32),
            pltpu.VMEM((PARTS, 8) + piece, BF16),
            pltpu.VMEM((PARTS,) + piece, BF16),
            pltpu.VMEM((PARTS, 4) + piece, BF16),
            pltpu.VMEM((PARTS * CH, W), BF16),
            pltpu.VMEM((NC, 2 * CH, W), BF16),
            pltpu.VMEM((NC, 8, 128), F32),
            pltpu.SemaphoreType.DMA((3,)),
            pltpu.SemaphoreType.DMA((PARTS, 3)),
            pltpu.SemaphoreType.DMA((PARTS, 3)),
            pltpu.SemaphoreType.DMA((2, 2)),
            pltpu.SemaphoreType.DMA((2, 2)),
            pltpu.SemaphoreType.DMA((2, 2)),
            pltpu.SemaphoreType.DMA((2,)),
        ],
        compiler_params=pltpu.CompilerParams(
            collective_id=0, has_side_effects=True, vmem_limit_bytes=56 * 2**20
        ),
        name="substitute",
    )(block_slot, target, ready, panel, rhs)
    return out.reshape(rows, width), mean


def solution(mesh):
    return jax.shard_map(
        per_device,
        mesh=mesh,
        in_specs=(P("row", None), P("row", "col"), P(), P(None, "col")),
        out_specs=(P("row", "col"), P("col")),
        check_vma=False,
    )
```

time: 55.2 us -> 57.6 us (1.043); the launches traced: 55.1 us -> 56.9 us
  Pallas kernels: 51.9 us -> 53.6 us
    pallas_call x0 -> x1, Pallas kernels: none -> 1 us  [per_device(): pl.pallas_call(prepare, out_shape=pltpu.VMEM((PARTS * CH, W), BF16), in_s...]
    pallas_call x1, Pallas kernels: 51.9 us -> 52.6 us  [per_device(): pl.pallas_call(kernel, out_shape=(pltpu.VMEM((rows // B, B, width), F32),...]
where the time goes in v4:
time: 57.6 us; the launch traced here: 56.9 us
  Pallas kernels  53.6 us (93%)
  local copies, waits for them, and re-layouts  2.58 us (4%)
  between operations  0.65 us (1%)
    pallas_call x1, Pallas kernels, per_device(): pl.pallas_call(kernel, out_shape=(pltpu.VMEM((rows // B, B, width), F32),...  52.6 us
    unnamed x4, local copies, waits for them, and re-layouts  2.58 us

profile of v4, /device:TPU:6, one launch (start us, length us, event | category | flops | bytes accessed | tf_op | source)
XLA Modules:
  0.0 56.9 jit_solution(15728657717738682781)
XLA Ops:
  0.6 1.0 %prepare.1.x_send = bf16[2560,256]{1,0:T(8,128)(2,1)S(1)} custom-call(s32[128]{0:T(128)} %slot_ref.3, bf16[4096,2048]{1,0:T(8,128)(2,1)} %panel_hbm.3, f32[4096,256]{1,0:T(8,128)} %rhs_hbm.3), custom_call_target="tpu_custom_call" | custom-call | tf_op jit(solution)/shard_map/prepare/pallas_call | solution.py:408
  1.6 52.6 %substitute.1 = (f32[4,1024,256]{2,1,0:T(8,128)S(1)}, f32[256]{0:T(256)}) custom-call(s32[128]{0:T(128)} %slot_ref.3, f32[2,128]{1,0:T(2,128)} %target_ref.1, bf16[2560,256]{1,0:T(8,128)(2,1)S(1)} %prepare.1.x_send, bf16[4096,2048]{1,0:T(8,128)(2,1)} %panel_hbm.3, f32[4096,256]{1,0:T(8,128)} %rhs_hbm.3), custom_call_target="tpu_custom_call" | custom-call | tf_op jit(solution)/shard_map/substitute/pallas_call | solution.py:430
  54.3 0.0 copy-start
  54.3 2.0 %copy.8 = f32[4096,256]{1,0:T(8,128)} copy(f32[4096,256]{1,0:T(8,128)S(1)} %bitcast.1) | data formatting | bytes 8388608
  56.3 0.0 copy-done
  56.3 0.6 copy.9
Async XLA Ops:
  54.3 2.0 %copy-start = (f32[256]{0:T(256)S(1)}, f32[256]{0:T(256)}, u32[]{:S(2)}) copy-start(f32[256]{0:T(256)} %get-tuple-element.11) | copy-start | bytes 3076

commit v5 on v3

--- a/solution.py
+++ b/solution.py
@@ -141,9 +141,10 @@
 
 
 def kernel(
-    slot_ref, target_ref, panel_hbm, rhs_hbm,
-    state, mean_ref,
-    panel_0, panel_1, low_0, diag_0, diag_1, work, inv_hi, inv_lo, solved, x_send, near_recv, z_send, z_recv, tgt,
+    slot_hbm, target_hbm, panel_hbm, rhs_hbm,
+    state, panel_1, done, mean_ref, code,
+    slot_ref, target_ref,
+    panel_0, low_0, diag_0, diag_1, work, inv_hi, inv_lo, solved, x_send, near_recv, z_send, z_recv, tgt,
     load_sem, send_sem, recv_sem, tgt_send, tgt_recv,
 ):
     row, col = lax.axis_index("row"), lax.axis_index("col")
@@ -165,13 +166,9 @@
     z_peers = [(y * NZ + lax.rem(z + d, NZ), col) for d in along]
     c_peers = [(row, lax.rem(col + d, NC)) for d in range(1, NC)]
     tgt[...] = jnp.zeros_like(tgt)
-    tgt[col, 0:2, :] = target_ref[...]
     barrier = pltpu.get_barrier_semaphore()
     near_peers = [near(0, dy, flip) for dy, flip in around] + [near(1, dy, flip) for dy, flip in around if flip]
     peers = near_peers + z_peers + c_peers
-    for peer in peers:
-        pl.semaphore_signal(barrier, inc=1, device_id=peer, device_id_type=MESH)
-
     def load(src, dst, k):
         copy = pltpu.make_async_copy(src, dst, load_sem.at[k])
         copy.start()
@@ -193,14 +190,24 @@
         for t in range(blocks):
             load(panel_hbm.at[pl.ds(t * B, B), pl.ds(k * B, B)], panel[k].at[t], sem)
 
-    lower = [(b, a) for b in range(NCH) for a in range(b)]
+    strip_at = [0, 3 * CH, 5 * CH]
     load_diag(0, 0)
+    load(slot_hbm, slot_ref, 6)
+    load(target_hbm, target_ref, 7)
+    for peer in peers:
+        pl.semaphore_signal(barrier, inc=1, device_id=peer, device_id_type=MESH)
     for t in range(blocks):
         load(rhs_hbm.at[pl.ds(t * B, B)], state.at[t], 1)
     for t in range(blocks):
-        for i, (b, a) in enumerate(lower):
-            load(panel_hbm.at[pl.ds(t * B + b * CH, CH), pl.ds(a * CH, CH)], low_0.at[t, i], 5)
-
+        for a in range(NCH - 1):
+            count = (NCH - 1 - a) * CH
+            load(
+                panel_hbm.at[pl.ds(t * B + (a + 1) * CH, count), pl.ds(a * CH, CH)],
+                low_0.at[t, pl.ds(strip_at[a], count)],
+                5,
+            )
+
+    pltpu.make_async_copy(slot_hbm, slot_ref, load_sem.at[6]).wait()
     mine = [slot_ref[0] // blocks == row, slot_ref[1] // blocks == row]
     local = [slot_ref[0] % blocks, slot_ref[1] % blocks]
 
@@ -227,7 +234,7 @@
             part = work[pl.ds(b * CH, CH), :]
             for a in range(b):
                 if k == 0:
-                    tile = low_0[local[0], lower.index((b, a))]
+                    tile = low_0[local[0], pl.ds(strip_at[a] + (b - a - 1) * CH, CH), :]
                 else:
                     tile = panel_1[local[1], pl.ds(b * CH, CH), pl.ds(a * CH, CH)]
                 part = part - (dot(tile, his[a]) + dot(tile, los[a]))
@@ -241,11 +248,6 @@
             x_send[k, pl.ds(b * CH, CH), :] = masked
             if k == 0 and b == 0:
                 pl.semaphore_wait(barrier, len(peers))
-                for peer in c_peers:
-                    pltpu.make_async_remote_copy(
-                        src_ref=tgt.at[col], dst_ref=tgt.at[col], send_sem=tgt_send, recv_sem=tgt_recv,
-                        device_id=peer, device_id_type=MESH,
-                    ).start()
             for dy, flip in around:
                 send(x_send.at[k, near_rows(b, dy, flip)], near_recv.at[k, b, dy * 2 + flip], k, b, 0, near(b, dy, flip))
 
@@ -274,20 +276,27 @@
         arrived(near_recv.at[k, c, pl.ds(1, 7)], k, c, 2)
 
     wait_load(diag_0, 0)
-    load_diag(1, 3)
-    load_column(0, 2)
-    load_column(1, 4)
     invert(0)
     wait_load(state, 1)
     work[...] = state[local[0]]
     wait_load(low_0, 5)
     solve(0)
+    load_column(0, 2)
+    load_diag(1, 3)
+    load_column(1, 4)
+    pltpu.make_async_copy(target_hbm, target_ref, load_sem.at[7]).wait()
+    tgt[col, 0:2, :] = target_ref[...]
+    for peer in c_peers:
+        pltpu.make_async_remote_copy(
+            src_ref=tgt.at[col], dst_ref=tgt.at[col], send_sem=tgt_send, recv_sem=tgt_recv,
+            device_id=peer, device_id_type=MESH,
+        ).start()
     for c in range(NCH):
         reduce_near(0, c)
+    for c in range(NCH):
+        reduce_along(0, c)
     wait_load(diag_1, 3)
     invert(1)
-    for c in range(NCH):
-        reduce_along(0, c)
     work[...] = state[local[1]]
     wait_load(panel_0, 2)
     wait_load(panel_1, 4)
@@ -301,11 +310,7 @@
 
     def apply_second(t, c):
         part = pl.ds(c * CH, CH)
-        value = state[t] - dot(panel_1[t, :, part], solved[1, part, :])
-        if c == NCH - 1:
-            value = jnp.where(slot_ref[1] == row * blocks + t, solved[1].astype(F32), value)
-            value = jnp.where(slot_ref[0] == row * blocks + t, solved[0].astype(F32), value)
-        state[t] = value
+        state[t] = state[t] - dot(panel_1[t, :, part], solved[1, part, :])
 
     def mean_weights():
         rest = jnp.concatenate([tgt[d] for d in range(NC)], axis=1)
@@ -320,9 +325,9 @@
         return found[k : k + 1] + found[8 + k : 9 + k] + found[16 + k : 17 + k]
 
     apply_first(0)
+    apply_first(1)
     for c in range(NCH):
         reduce_near(1, c)
-    apply_first(1)
     apply_first(2)
     for c in range(NCH):
         reduce_along(1, c)
@@ -330,10 +335,18 @@
     pltpu.make_async_copy(tgt.at[pl.ds(0, NC - 1)], tgt.at[pl.ds(0, NC - 1)], tgt_recv).wait()
     weights = mean_weights()
     mean = mean_terms(weights, 0)
+    done[0] = solved[0]
+    kind = jnp.zeros((8, 128), jnp.int32)
+    for t in range(blocks):
+        here = [(slot_ref[i] == row * blocks + t).astype(jnp.int32) for i in range(2)]
+        kind = jnp.where(iota((8, 128), 0) == t, 2 * here[0] + here[1], kind)
+    code[...] = kind
     for c in range(NCH):
         gather(1, c)
-        for t in range(blocks):
-            apply_second(t, c)
+        done[1, pl.ds(c * CH, CH), :] = solved[1, pl.ds(c * CH, CH), :]
+        if c < NCH - 1:
+            for t in range(blocks):
+                apply_second(t, c)
     mean_ref[...] = (mean + mean_terms(weights, 1)).reshape(W)
 
     for k in range(2):
@@ -343,23 +356,49 @@
     pltpu.make_async_copy(tgt.at[pl.ds(0, NC - 1)], tgt.at[pl.ds(0, NC - 1)], tgt_send).wait()
 
 
+def finish(state, panel_1, done, mean, code, out_hbm, mean_hbm, stage, store_sem, mean_sem):
+    blocks, rows = 4, B // 2
+    last = pl.ds(B - CH, CH)
+    pltpu.make_async_copy(mean, mean_hbm, mean_sem).start()
+    for t in range(blocks):
+        kind = jnp.broadcast_to(code[t : t + 1, :], (rows, 128))
+        kind = jnp.concatenate([kind, kind], axis=1)
+        for i in range(2):
+            part = pl.ds(i * rows, rows)
+            value = state[t, part, :] - dot(panel_1[t, part, last], done[1, last, :])
+            value = jnp.where(kind == 1, done[1, part, :].astype(F32), value)
+            stage[t, part, :] = jnp.where(kind == 2, done[0, part, :].astype(F32), value)
+            pltpu.make_async_copy(
+                stage.at[t, part], out_hbm.at[pl.ds(t * B + i * rows, rows)], store_sem.at[t, i]
+            ).start()
+    for t in range(blocks):
+        for i in range(2):
+            part = pl.ds(i * rows, rows)
+            pltpu.make_async_copy(
+                stage.at[t, part], out_hbm.at[pl.ds(t * B + i * rows, rows)], store_sem.at[t, i]
+            ).wait()
+    pltpu.make_async_copy(mean, mean_hbm, mean_sem).wait()
+
+
 def per_device(panel, rhs, block_slot, target):
     rows, width = rhs.shape
     piece = (PIECE, W)
-    out, mean = pl.pallas_call(
+    held = pl.pallas_call(
         kernel,
-        out_shape=(pltpu.VMEM((rows // B, B, width), F32), jax.ShapeDtypeStruct((width,), F32)),
-        in_specs=[
-            pl.BlockSpec(memory_space=pltpu.SMEM),
-            pl.BlockSpec(memory_space=pltpu.VMEM),
-            pl.BlockSpec(memory_space=pl.ANY),
-            pl.BlockSpec(memory_space=pl.ANY),
-        ],
-        out_specs=(pl.BlockSpec(memory_space=pltpu.VMEM), pl.BlockSpec(memory_space=pltpu.VMEM)),
+        out_shape=(
+            pltpu.VMEM((rows // B, B, width), F32),
+            pltpu.VMEM((4, B, B), BF16),
+            pltpu.VMEM((2, B, W), BF16),
+            pltpu.VMEM((width,), F32),
+            pltpu.VMEM((8, 128), jnp.int32),
+        ),
+        in_specs=[pl.BlockSpec(memory_space=pl.ANY)] * 4,
+        out_specs=(pl.BlockSpec(memory_space=pltpu.VMEM),) * 5,
         scratch_shapes=[
+            pltpu.SMEM((128,), jnp.int32),
+            pltpu.VMEM((2, 128), F32),
             pltpu.VMEM((4, B, B), BF16),
-            pltpu.VMEM((4, B, B), BF16),
-            pltpu.VMEM((4, 6, CH, CH), BF16),
+            pltpu.VMEM((4, 6 * CH, CH), BF16),
             pltpu.VMEM((4, B, CH), BF16),
             pltpu.VMEM((4, B, CH), BF16),
             pltpu.VMEM((B, W), F32),
@@ -371,18 +410,27 @@
             pltpu.VMEM((2, NCH) + piece, BF16),
             pltpu.VMEM((2, NCH, 4) + piece, BF16),
             pltpu.VMEM((NC, 8, 128), F32),
-            pltpu.SemaphoreType.DMA((6,)),
+            pltpu.SemaphoreType.DMA((8,)),
             pltpu.SemaphoreType.DMA((2, NCH, 3)),
             pltpu.SemaphoreType.DMA((2, NCH, 3)),
             pltpu.SemaphoreType.DMA,
             pltpu.SemaphoreType.DMA,
         ],
         compiler_params=pltpu.CompilerParams(
-            collective_id=0, has_side_effects=True, vmem_limit_bytes=56 * 2**20
+            collective_id=0, has_side_effects=True, vmem_limit_bytes=44 * 2**20
         ),
         name="substitute",
     )(block_slot, target, panel, rhs)
-    return out.reshape(rows, width), mean
+    held = [pltpu.with_memory_space_constraint(v, pltpu.VMEM) for v in held]
+    return pl.pallas_call(
+        finish,
+        out_shape=(jax.ShapeDtypeStruct((rows, width), F32), jax.ShapeDtypeStruct((width,), F32)),
+        in_specs=[pl.BlockSpec(memory_space=pltpu.VMEM)] * 5,
+        out_specs=(pl.BlockSpec(memory_space=pl.ANY),) * 2,
+        scratch_shapes=[pltpu.VMEM((4, B, W), F32), pltpu.SemaphoreType.DMA((4, 2)), pltpu.SemaphoreType.DMA],
+        compiler_params=pltpu.CompilerParams(vmem_limit_bytes=20 * 2**20),
+        name="finish",
+    )(*held)
 
 
 def solution(mesh):

time: 55.2 us -> 52.8 us (0.957)
  local copies, waits for them, and re-layouts: 2.58 us -> 0 us
    unnamed x4 -> x0, local copies, waits for them, and re-layouts: 2.58 us -> none
    pallas_call x0 -> x1, Pallas kernels: none -> 2.5 us  [per_device(): pl.pallas_call(finish, out_shape=(jax.ShapeDtypeStruct((rows, width), F32...]
    pallas_call x1, Pallas kernels: 51.9 us -> 49.4 us  [per_device(): pl.pallas_call(kernel, out_shape=(pltpu.VMEM((rows // B, B, width), F32),...]
where the time goes in v5:
time: 52.8 us; the launch traced here: 52.5 us
  Pallas kernels  51.9 us (98%)
  between operations  0.64 us (1%)
    pallas_call x1, Pallas kernels, per_device(): pl.pallas_call(kernel, out_shape=(pltpu.VMEM((rows // B, B, width), F32),...  49.4 us
    pallas_call x1, Pallas kernels, per_device(): pl.pallas_call(finish, out_shape=(jax.ShapeDtypeStruct((rows, width), F32...  2.5 us

profile of v5, /device:TPU:6, one launch (start us, length us, event | category | flops | bytes accessed | tf_op | source)
XLA Modules:
  0.0 52.5 jit_solution(17740609331249765243)
XLA Ops:
  0.6 49.4 %substitute.1 = (f32[4,1024,256]{2,1,0:T(8,128)S(1)}, bf16[4,1024,1024]{2,1,0:T(8,128)(2,1)S(1)}, bf16[2,1024,256]{2,1,0:T(8,128)(2,1)S(1)}, f32[256]{0:T(256)S(1)}, s32[8,128]{1,0:T(8,128)S(1)}) custom-call(s32[128]{0:T(128)} %slot_hbm.1, f32[2,128]{1,0:T(2,128)} %target_hbm.1, bf16[4096,2048]{1,0:T(8,128)(2,1)} %panel_hbm.1, f32[4096,256]{1,0:T(8,128)} %rhs_hbm.1), custom_call_target="tpu_custom_call" | custom-call | tf_op jit(solution)/shard_map/substitute/pallas_call | solution.py:386
  50.0 2.5 %finish.1 = (f32[4096,256]{1,0:T(8,128)}, f32[256]{0:T(256)}) custom-call(f32[4,1024,256]{2,1,0:T(8,128)S(1)} %get-tuple-element.7.state, bf16[4,1024,1024]{2,1,0:T(8,128)(2,1)S(1)} %get-tuple-element.8.panel_1, bf16[2,1024,256]{2,1,0:T(8,128)(2,1)S(1)} %get-tuple-element.9.done, f32[256]{0:T(256)S(1)} %get-tuple-element.10.mean, ...), custom_call_target="tpu_custom_call" | custom-call | tf_op jit(solution)/shard_map/finish/pallas_call | solution.py:425

commit v6 on v5

--- a/solution.py
+++ b/solution.py
@@ -62,10 +62,8 @@
     return [x[g] for g in range(groups)]
 
 
-def join_inverses(diag_block):
-    groups = B // 128
-    spread = spread_matrix()
-    blocks = [diag_block(g) for g in range(groups)]
+def join_inverses(blocks, spread):
+    groups = len(blocks)
     small = invert_small(blocks, spread)
     r, c = iota((128, 128), 0), iota((128, 128), 1)
     inverses = []
@@ -144,7 +142,7 @@
     slot_hbm, target_hbm, panel_hbm, rhs_hbm,
     state, panel_1, done, mean_ref, code,
     slot_ref, target_ref,
-    panel_0, low_0, diag_0, diag_1, work, inv_hi, inv_lo, solved, x_send, near_recv, z_send, z_recv, tgt,
+    spread_ref, panel_0, low_0, diag_a, diag_b, diag_1, work, inv_hi, inv_lo, solved, x_send, near_recv, z_send, z_recv, tgt,
     load_sem, send_sem, recv_sem, tgt_send, tgt_recv,
 ):
     row, col = lax.axis_index("row"), lax.axis_index("col")
@@ -175,14 +173,14 @@
         return copy
 
     blocks = 4
-    panel, diag = [panel_0, panel_1], [diag_0, diag_1]
-
-    def load_diag(k, sem):
+    panel = [panel_0, panel_1]
+
+    def load_diag(k, parts, dst, sem):
         for t in range(blocks):
-            for b in range(NCH):
+            for i, b in enumerate(parts):
                 load(
                     panel_hbm.at[pl.ds(t * B + b * CH, CH), pl.ds(k * B + b * CH, CH)],
-                    diag[k].at[t, pl.ds(b * CH, CH)],
+                    dst.at[t, pl.ds(i * CH, CH)],
                     sem,
                 )
 
@@ -191,13 +189,14 @@
             load(panel_hbm.at[pl.ds(t * B, B), pl.ds(k * B, B)], panel[k].at[t], sem)
 
     strip_at = [0, 3 * CH, 5 * CH]
-    load_diag(0, 0)
+    load_diag(0, [0, 1], diag_a, 0)
     load(slot_hbm, slot_ref, 6)
     load(target_hbm, target_ref, 7)
     for peer in peers:
         pl.semaphore_signal(barrier, inc=1, device_id=peer, device_id_type=MESH)
     for t in range(blocks):
         load(rhs_hbm.at[pl.ds(t * B, B)], state.at[t], 1)
+    load_diag(0, [2, 3], diag_b, 8)
     for t in range(blocks):
         for a in range(NCH - 1):
             count = (NCH - 1 - a) * CH
@@ -207,6 +206,7 @@
                 5,
             )
 
+    spread_ref[...] = spread_matrix()
     pltpu.make_async_copy(slot_hbm, slot_ref, load_sem.at[6]).wait()
     mine = [slot_ref[0] // blocks == row, slot_ref[1] // blocks == row]
     local = [slot_ref[0] % blocks, slot_ref[1] % blocks]
@@ -214,12 +214,13 @@
     def wait_load(ref, k):
         pltpu.make_async_copy(ref, ref, load_sem.at[k]).wait()
 
-    def invert(k):
-        found = join_inverses(
-            lambda g: diag[k][local[k], pl.ds(128 * g, 128), pl.ds(128 * (g % 2), 128)]
-        )
-        corners = [diag[k][local[k], pl.ds(CH * b + 128, 128), pl.ds(0, 128)] for b in range(NCH)]
-        for b, (hi, lo) in enumerate(whole_inverses(found, corners)):
+    def invert(k, parts):
+        def diagonal(b, r, c):
+            buf = diag_1 if k else (diag_a if b < 2 else diag_b)
+            return buf[local[k], pl.ds((b if k else b % 2) * CH + r, 128), pl.ds(c, 128)]
+
+        found = join_inverses([diagonal(b, r, r) for b in parts for r in (0, 128)], spread_ref[...])
+        for b, (hi, lo) in zip(parts, whole_inverses(found, [diagonal(b, 128, 0) for b in parts])):
             inv_hi[b], inv_lo[b] = hi, lo
 
     def send(src, dst, k, c, stage, peer):
@@ -231,7 +232,16 @@
     def solve(k):
         his, los = [], []
         for b in range(NCH):
-            part = work[pl.ds(b * CH, CH), :]
+            if k == 0 and b == 1:
+                wait_load(low_0, 5)
+            if k == 0 and b == 2:
+                wait_load(diag_b, 8)
+                invert(0, [2, 3])
+            rows, last = pl.ds(b * CH, CH), pl.ds(B - CH, CH)
+            if k == 0:
+                part = state[local[0], rows, :]
+            else:
+                part = work[rows, :] - dot(panel_0[local[1], rows, last], solved[0, last, :])
             for a in range(b):
                 if k == 0:
                     tile = low_0[local[0], pl.ds(strip_at[a] + (b - a - 1) * CH, CH), :]
@@ -275,14 +285,12 @@
     def gather(k, c):
         arrived(near_recv.at[k, c, pl.ds(1, 7)], k, c, 2)
 
-    wait_load(diag_0, 0)
-    invert(0)
+    wait_load(diag_a, 0)
+    invert(0, [0, 1])
     wait_load(state, 1)
-    work[...] = state[local[0]]
-    wait_load(low_0, 5)
     solve(0)
     load_column(0, 2)
-    load_diag(1, 3)
+    load_diag(1, range(NCH), diag_1, 3)
     load_column(1, 4)
     pltpu.make_async_copy(target_hbm, target_ref, load_sem.at[7]).wait()
     tgt[col, 0:2, :] = target_ref[...]
@@ -296,12 +304,14 @@
     for c in range(NCH):
         reduce_along(0, c)
     wait_load(diag_1, 3)
-    invert(1)
+    invert(1, range(NCH))
     work[...] = state[local[1]]
     wait_load(panel_0, 2)
     wait_load(panel_1, 4)
     for c in range(NCH):
         gather(0, c)
+        if c == NCH - 1:
+            break
         work[...] = work[...] - dot(panel_0[local[1], :, pl.ds(c * CH, CH)], solved[0, pl.ds(c * CH, CH), :])
     solve(1)
 
@@ -397,9 +407,11 @@
         scratch_shapes=[
             pltpu.SMEM((128,), jnp.int32),
             pltpu.VMEM((2, 128), F32),
+            pltpu.VMEM((128, BASE * 128), BF16),
             pltpu.VMEM((4, B, B), BF16),
             pltpu.VMEM((4, 6 * CH, CH), BF16),
-            pltpu.VMEM((4, B, CH), BF16),
+            pltpu.VMEM((4, 2 * CH, CH), BF16),
+            pltpu.VMEM((4, 2 * CH, CH), BF16),
             pltpu.VMEM((4, B, CH), BF16),
             pltpu.VMEM((B, W), F32),
             pltpu.VMEM((NCH, CH, CH), BF16),
@@ -410,7 +422,7 @@
             pltpu.VMEM((2, NCH) + piece, BF16),
             pltpu.VMEM((2, NCH, 4) + piece, BF16),
             pltpu.VMEM((NC, 8, 128), F32),
-            pltpu.SemaphoreType.DMA((8,)),
+            pltpu.SemaphoreType.DMA((9,)),
             pltpu.SemaphoreType.DMA((2, NCH, 3)),
             pltpu.SemaphoreType.DMA((2, NCH, 3)),
             pltpu.SemaphoreType.DMA,

time: 52.8 us -> 52.1 us (0.987)
    pallas_call x1, Pallas kernels: 49.4 us -> 48.9 us  [per_device(): pl.pallas_call(kernel, out_shape=(pltpu.VMEM((rows // B, B, width), F32),...]
where the time goes in v6:
time: 52.1 us; the launch traced here: 52 us
  Pallas kernels  51.4 us (99%)
  between operations  0.64 us (1%)
    pallas_call x1, Pallas kernels, per_device(): pl.pallas_call(kernel, out_shape=(pltpu.VMEM((rows // B, B, width), F32),...  48.9 us
    pallas_call x1, Pallas kernels, per_device(): pl.pallas_call(finish, out_shape=(jax.ShapeDtypeStruct((rows, width), F32...  2.49 us

profile of v6, /device:TPU:6, one launch (start us, length us, event | category | flops | bytes accessed | tf_op | source)
XLA Modules:
  0.0 52.0 jit_solution(9328849383643175629)
XLA Ops:
  0.6 48.9 %substitute.1 = (f32[4,1024,256]{2,1,0:T(8,128)S(1)}, bf16[4,1024,1024]{2,1,0:T(8,128)(2,1)S(1)}, bf16[2,1024,256]{2,1,0:T(8,128)(2,1)S(1)}, f32[256]{0:T(256)S(1)}, s32[8,128]{1,0:T(8,128)S(1)}) custom-call(s32[128]{0:T(128)} %slot_hbm.1, f32[2,128]{1,0:T(2,128)} %target_hbm.1, bf16[4096,2048]{1,0:T(8,128)(2,1)} %panel_hbm.1, f32[4096,256]{1,0:T(8,128)} %rhs_hbm.1), custom_call_target="tpu_custom_call" | custom-call | tf_op jit(solution)/shard_map/substitute/pallas_call | solution.py:396
  49.5 2.5 %finish.1 = (f32[4096,256]{1,0:T(8,128)}, f32[256]{0:T(256)}) custom-call(f32[4,1024,256]{2,1,0:T(8,128)S(1)} %get-tuple-element.7.state, bf16[4,1024,1024]{2,1,0:T(8,128)(2,1)S(1)} %get-tuple-element.8.panel_1, bf16[2,1024,256]{2,1,0:T(8,128)(2,1)S(1)} %get-tuple-element.9.done, f32[256]{0:T(256)S(1)} %get-tuple-element.10.mean, ...), custom_call_target="tpu_custom_call" | custom-call | tf_op jit(solution)/shard_map/finish/pallas_call | solution.py:437

commit v7 on v6

--- a/solution.py
+++ b/solution.py
@@ -149,7 +149,7 @@
     y, z = row // NZ, row % NZ
 
     def half(c):
-        return lax.rem(z + c % 2, 2)
+        return lax.rem(z, 2)
 
     def near(c, dy, flip):
         step = flip * (1 - 2 * half(c))
@@ -165,7 +165,7 @@
     c_peers = [(row, lax.rem(col + d, NC)) for d in range(1, NC)]
     tgt[...] = jnp.zeros_like(tgt)
     barrier = pltpu.get_barrier_semaphore()
-    near_peers = [near(0, dy, flip) for dy, flip in around] + [near(1, dy, flip) for dy, flip in around if flip]
+    near_peers = [near(0, dy, flip) for dy, flip in around]
     peers = near_peers + z_peers + c_peers
     def load(src, dst, k):
         copy = pltpu.make_async_copy(src, dst, load_sem.at[k])

time: 52.1 us -> 52.9 us (1.015)
  Pallas kernels: 51.4 us -> 52.2 us
    pallas_call x1, Pallas kernels: 48.9 us -> 49.7 us  [per_device(): pl.pallas_call(kernel, out_shape=(pltpu.VMEM((rows // B, B, width), F32),...]
where the time goes in v7:
time: 52.9 us; the launch traced here: 52.8 us
  Pallas kernels  52.2 us (99%)
  between operations  0.64 us (1%)
    pallas_call x1, Pallas kernels, per_device(): pl.pallas_call(kernel, out_shape=(pltpu.VMEM((rows // B, B, width), F32),...  49.7 us
    pallas_call x1, Pallas kernels, per_device(): pl.pallas_call(finish, out_shape=(jax.ShapeDtypeStruct((rows, width), F32...  2.48 us

profile of v7, /device:TPU:6, one launch (start us, length us, event | category | flops | bytes accessed | tf_op | source)
XLA Modules:
  0.0 52.8 jit_solution(18320871634964725977)
XLA Ops:
  0.6 49.7 %substitute.1 = (f32[4,1024,256]{2,1,0:T(8,128)S(1)}, bf16[4,1024,1024]{2,1,0:T(8,128)(2,1)S(1)}, bf16[2,1024,256]{2,1,0:T(8,128)(2,1)S(1)}, f32[256]{0:T(256)S(1)}, s32[8,128]{1,0:T(8,128)S(1)}) custom-call(s32[128]{0:T(128)} %slot_hbm.1, f32[2,128]{1,0:T(2,128)} %target_hbm.1, bf16[4096,2048]{1,0:T(8,128)(2,1)} %panel_hbm.1, f32[4096,256]{1,0:T(8,128)} %rhs_hbm.1), custom_call_target="tpu_custom_call" | custom-call | tf_op jit(solution)/shard_map/substitute/pallas_call | solution.py:396
  50.3 2.5 %finish.1 = (f32[4096,256]{1,0:T(8,128)}, f32[256]{0:T(256)}) custom-call(f32[4,1024,256]{2,1,0:T(8,128)S(1)} %get-tuple-element.7.state, bf16[4,1024,1024]{2,1,0:T(8,128)(2,1)S(1)} %get-tuple-element.8.panel_1, bf16[2,1024,256]{2,1,0:T(8,128)(2,1)S(1)} %get-tuple-element.9.done, f32[256]{0:T(256)S(1)} %get-tuple-element.10.mean, ...), custom_call_target="tpu_custom_call" | custom-call | tf_op jit(solution)/shard_map/finish/pallas_call | solution.py:437
